TPU v7x, 32 devices: a whole 2x2x4 slice. The times are simulated.
32 devices in a mesh: section: 4 (over y, x), expert: 8 (over z, core).
Axes of the slice: x: 2, y: 2, z: 4, core: 2. Of those that a mesh axis runs over, the one named last changes fastest.
Arguments:
- embedded: bfloat16 [4, 128, 7168], P('section', 'expert'), may hold values from -6 to 6
- norm_gain: float32 [4, 7168], P('section'), may hold values from 0.1 to 1.9
- gate_proj: bfloat16 [4, 7168, 2048], P('section', None, 'expert'), may hold values from -0.0625 to 0.0625
- up_proj: bfloat16 [4, 7168, 2048], P('section', None, 'expert'), may hold values from -0.0625 to 0.0625
- down_proj: bfloat16 [4, 2048, 7168], P('section', 'expert'), may hold values from -0.125 to 0.125
- expert_ids: int32 [4, 4, 128, 8], P('section', None, 'expert'), may hold values from 0 to 255, all different within a row; in each aligned block of 16 rows (0 to 15, 16 to 31, ..., all dimensions but the last counted through in order) at most 2 rows name the same one
- route_gates: float32 [4, 4, 128, 8], P('section', None, 'expert'), may hold values from 0.2 to 2.5
Outputs:
- processed: bfloat16 [4, 128, 7168], P('section', 'expert')
Inputs may be any that keep to these rules, and one draw needn't show every extreme that they name: `expert_ids`: each row names 8 different experts; within one layer and micro-batch no expert is named by more than 2 tokens of an aligned block of 16 tokens.
All inputs are finite; a program needn't handle non-finite values.
Results may differ from a plain program's by a relative error of at most 0.0085.
Values may be sent and summed in bfloat16 or wider, within the bound.
No kernel may reach another device: no remote copies, remote signals or barrier semaphores. Data moves between devices by JAX's collectives and lax.ppermute only.
A program may use at most 128 MiB of HBM per device.

v0:
```python
import jax
import jax.numpy as jnp
from jax import lax
from jax.sharding import PartitionSpec as P

CAP = 2


eps_norm = 1e-06


def from_behind(array, axis, by):
    devices = lax.axis_size(axis)
    pairs = [(i, i + by) for i in range(devices) if 0 <= i + by < devices]
    return lax.ppermute(array, axis, pairs)


def slot_table(chosen, num_experts):
    expert_range = jnp.arange(num_experts, dtype=jnp.int32)
    matched = (chosen[..., None] == expert_range).astype(jnp.int32)
    hit_table = jnp.sum(matched, axis=-2, dtype=jnp.int32)
    earlier = jnp.cumsum(hit_table, axis=-2, dtype=jnp.int32) - hit_table
    slot_index = jnp.sum(matched * earlier[..., None, :], axis=-1, dtype=jnp.int32)
    inside = chosen < num_experts
    return (slot_index, inside)


def place_mask(chosen, slot_index, inside, num_experts):
    flat_index = chosen * CAP + slot_index
    target = jnp.arange(num_experts * CAP, dtype=jnp.int32)
    return (flat_index[..., None] == target) & inside[..., None]


def moe_layer(rows, gain_row, gate_mat, up_mat, down_mat, chosen, weights_k):
    n_dev = lax.axis_size("expert")
    group_size = min(8, n_dev)
    num_experts = n_dev // group_size
    width_model = rows.shape[1]
    rows_float = rows.astype(jnp.float32)
    scale = lax.rsqrt(jnp.mean(rows_float * rows_float, axis=-1, keepdims=True) + eps_norm)
    normed = (rows_float * scale * gain_row).astype(jnp.bfloat16)
    slot_index, inside = slot_table(chosen, num_experts)
    placed = place_mask(chosen, slot_index, inside, num_experts)
    mask_any = jnp.any(placed, axis=1).astype(jnp.bfloat16)
    send_block = jnp.dot(mask_any.T, normed, preferred_element_type=jnp.float32).astype(
        jnp.bfloat16
    )
    send_block = send_block.reshape(num_experts, CAP, width_model)
    send_all = jnp.repeat(send_block, group_size, axis=0)
    received = lax.all_to_all(send_all, "expert", split_axis=0, concat_axis=0, tiled=True)
    rows_in = received.reshape(n_dev * CAP, width_model)
    gate_val = jnp.dot(rows_in, gate_mat, preferred_element_type=jnp.float32)
    up_val = jnp.dot(rows_in, up_mat, preferred_element_type=jnp.float32)
    hidden = (jax.nn.silu(gate_val) * up_val).astype(jnp.bfloat16)
    partial_value = jnp.dot(hidden, down_mat, preferred_element_type=jnp.float32).astype(
        jnp.bfloat16
    )
    returned = lax.all_to_all(
        partial_value.reshape(n_dev, CAP, width_model),
        "expert",
        split_axis=0,
        concat_axis=0,
        tiled=True,
    )
    expert_out = jnp.sum(
        returned.reshape(num_experts, group_size, CAP, width_model).astype(jnp.float32), axis=1
    )
    expert_out = expert_out.reshape(num_experts * CAP, width_model)
    weight_table = jnp.sum(jnp.where(placed, weights_k[:, :, None], 0.0), axis=1)
    routed_sum = jnp.dot(
        weight_table,
        expert_out,
        precision=lax.Precision.HIGHEST,
        preferred_element_type=jnp.float32,
    )
    return (rows_float + routed_sum).astype(jnp.bfloat16)


def shards(embedded, norm_gain, gate_proj, up_proj, down_proj, expert_ids, route_gates):
    n_section = lax.axis_size("section")
    section_pos = lax.axis_index("section")
    micro_count = expert_ids.shape[1]
    steps_total = micro_count + n_section - 1
    own_block = embedded[0]
    carry_rows = jnp.zeros_like(own_block)
    every_block = lax.all_gather(embedded, "section", axis=0, tiled=True)
    finished = jnp.zeros_like(every_block)
    for moment in range(steps_total):
        micro_pos = moment - section_pos
        clipped = jnp.clip(micro_pos, 0, micro_count - 1)
        chosen = lax.dynamic_index_in_dim(expert_ids[0], clipped, 0, keepdims=False)
        weights_k = lax.dynamic_index_in_dim(route_gates[0], clipped, 0, keepdims=False)
        if moment < micro_count:
            fresh_rows = every_block[moment]
        else:
            fresh_rows = jnp.zeros_like(own_block)
        layer_in = jnp.where(section_pos == 0, fresh_rows, carry_rows)
        layer_out = moe_layer(
            layer_in, norm_gain[0], gate_proj[0], up_proj[0], down_proj[0], chosen, weights_k
        )
        if moment >= n_section - 1:
            finished = finished.at[moment - n_section + 1].set(layer_out)
        if moment < steps_total - 1:
            carry_rows = from_behind(layer_out, "section", 1)
    spread = lax.all_to_all(finished, "section", split_axis=0, concat_axis=0, tiled=True)
    result = spread[n_section - 1]
    return result[None]


def solution(mesh):
    placed = (
        P("section", "expert", None),
        P("section", None),
        P("section", None, "expert"),
        P("section", None, "expert"),
        P("section", "expert", None),
        P("section", None, "expert", None),
        P("section", None, "expert", None),
    )
    return jax.shard_map(
        shards, mesh=mesh, in_specs=placed, out_specs=P("section", "expert", None), check_vma=False
    )
```

profile of v0, /device:TPU:0, one launch (start us, length us, event | category | flops | bytes accessed | tf_op | source)
XLA Modules:
  0.0 335.0 jit_solution(10605652477697006222)
XLA Ops:
  2.2 14.9 %all_gather.3 = bf16[4,16,7168]{2,1,0:T(8,128)(2,1)S(1)} all-gather(bf16[1,16,7168]{2,1,0:T(8,128)(2,1)} %param.15), channel_id=1, replica_groups=mesh['section'=4,'expert'=8] {'section'}, dimensions={0}, use_global_device_ids=true | all-gather | bytes 1146880 | tf_op jit(solution)/shard_map/all_gather | solution.py:86
  19.1 13.7 %all_to_all.75 = bf16[8,2,7168]{2,1,0:T(2,128)(2,1)S(1)} all-to-all(bf16[8,2,7168]{2,1,0:T(2,128)(2,1)S(1)} %reshape.1031), channel_id=1, replica_groups=mesh['section'=4,'expert'=8] {'expert'}, dimensions={0} | all-to-all | bytes 458752 | tf_op jit(solution)/shard_map/all_to_all | solution.py:50
  35.6 5.3 %convolution_convert_fusion.6 = bf16[16,7168]{1,0:T(8,128)(2,1)S(1)} fusion(bf16[1,256,7168]{2,1,0:T(8,128)(2,1)} %param.19, bf16[16,7168]{1,0:T(8,128)(2,1)S(1)} %reshape.1032, bf16[1,7168,256]{2,1,0:T(8,128)(2,1)} %param.18, f32[16,256]{1,0:T(8,128)S(1)} %fusion.42), kind=kOutput, calls=%fused_computation.20 | convolution fusion | flops 117579776 | bytes 7815168 | tf_op jit(solution)/shard_map/dot_general | solution.py:55
  46.4 7.7 %all-to-all-done.1 = bf16[8,2,7168]{2,1,0:T(2,128)(2,1)S(1)} async-done(((bf16[8,2,7168]{2,1,0:T(2,128)(2,1)}), bf16[8,2,7168]{2,1,0:T(2,128)(2,1)S(1)}, u32[]{:S(2)}, u32[]{:S(2)}) %all-to-all-start.1) | async-done | bytes 229408 | tf_op jit(solution)/shard_map/all_to_all | solution.py:58
  57.3 4.4 %collective-permute-done = bf16[16,7168]{1,0:T(8,128)(2,1)S(1)} collective-permute-done((bf16[16,7168]{1,0:T(8,128)(2,1)S(1)}, bf16[16,7168]{1,0:T(8,128)(2,1)S(1)}, u32[]{:S(2)}, u32[]{:S(2)}) %collective-permute-start) | collective-permute-done | bytes 229408 | tf_op jit(solution)/shard_map/ppermute | solution.py:15
  62.4 11.9 %all_to_all.76 = bf16[8,2,7168]{2,1,0:T(2,128)(2,1)S(1)} all-to-all(bf16[8,2,7168]{2,1,0:T(2,128)(2,1)S(1)} %reshape.1036), channel_id=1, replica_groups=mesh['section'=4,'expert'=8] {'expert'}, dimensions={0} | all-to-all | bytes 458752 | tf_op jit(solution)/shard_map/all_to_all | solution.py:50
  77.0 5.2 %convolution_convert_fusion.5 = bf16[16,7168]{1,0:T(8,128)(2,1)S(1)} fusion(bf16[1,256,7168]{2,1,0:T(8,128)(2,1)} %param.19, bf16[16,7168]{1,0:T(8,128)(2,1)S(1)} %reshape.1037, bf16[1,7168,256]{2,1,0:T(8,128)(2,1)} %param.18, f32[16,256]{1,0:T(8,128)S(1)} %fusion.40), kind=kOutput, calls=%fused_computation.19 | convolution fusion | flops 117579776 | bytes 7815168 | tf_op jit(solution)/shard_map/dot_general | solution.py:55
  86.5 8.9 %all-to-all-done.3 = bf16[8,2,7168]{2,1,0:T(2,128)(2,1)S(1)} async-done(((bf16[8,2,7168]{2,1,0:T(2,128)(2,1)}), bf16[8,2,7168]{2,1,0:T(2,128)(2,1)S(1)}, u32[]{:S(2)}, u32[]{:S(2)}) %all-to-all-start.3) | async-done | bytes 229408 | tf_op jit(solution)/shard_map/all_to_all | solution.py:58
  100.7 4.5 %collective-permute-done.1 = bf16[16,7168]{1,0:T(8,128)(2,1)S(1)} collective-permute-done((bf16[16,7168]{1,0:T(8,128)(2,1)S(1)}, bf16[16,7168]{1,0:T(8,128)(2,1)S(1)}, u32[]{:S(2)}, u32[]{:S(2)}) %collective-permute-start.1) | collective-permute-done | bytes 229408 | tf_op jit(solution)/shard_map/ppermute | solution.py:15
  105.7 11.9 %all_to_all.77 = bf16[8,2,7168]{2,1,0:T(2,128)(2,1)S(1)} all-to-all(bf16[8,2,7168]{2,1,0:T(2,128)(2,1)S(1)} %reshape.1041), channel_id=1, replica_groups=mesh['section'=4,'expert'=8] {'expert'}, dimensions={0} | all-to-all | bytes 458752 | tf_op jit(solution)/shard_map/all_to_all | solution.py:50
  120.4 5.2 %convolution_convert_fusion.4 = bf16[16,7168]{1,0:T(8,128)(2,1)S(1)} fusion(bf16[1,256,7168]{2,1,0:T(8,128)(2,1)} %param.19, bf16[16,7168]{1,0:T(8,128)(2,1)S(1)} %reshape.1042, bf16[1,7168,256]{2,1,0:T(8,128)(2,1)} %param.18, f32[16,256]{1,0:T(8,128)S(1)} %fusion.38), kind=kOutput, calls=%fused_computation.18 | convolution fusion | flops 117579776 | bytes 7815168 | tf_op jit(solution)/shard_map/dot_general | solution.py:55
  129.8 8.9 %all-to-all-done.5 = bf16[8,2,7168]{2,1,0:T(2,128)(2,1)S(1)} async-done(((bf16[8,2,7168]{2,1,0:T(2,128)(2,1)}), bf16[8,2,7168]{2,1,0:T(2,128)(2,1)S(1)}, u32[]{:S(2)}, u32[]{:S(2)}) %all-to-all-start.5) | async-done | bytes 229408 | tf_op jit(solution)/shard_map/all_to_all | solution.py:58
  139.6 4.6 %collective-permute-start.2 = (bf16[16,7168]{1,0:T(8,128)(2,1)S(1)}, bf16[16,7168]{1,0:T(8,128)(2,1)S(1)}, u32[]{:S(2)}, u32[]{:S(2)}) collective-permute-start(bf16[16,7168]{1,0:T(8,128)(2,1)S(1)} %fusion.2), channel_id=1, source_target_pairs={{0,8},{8,16},{16,24},{1,9},{9,17},{17,25},{2,10},{10,18},{18,26},{... | collective-permute-start | bytes 688136 | tf_op jit(solution)/shard_map/ppermute | solution.py:15
  149.1 11.9 %all_to_all.78 = bf16[8,2,7168]{2,1,0:T(2,128)(2,1)S(1)} all-to-all(bf16[8,2,7168]{2,1,0:T(2,128)(2,1)S(1)} %reshape.1046), channel_id=1, replica_groups=mesh['section'=4,'expert'=8] {'expert'}, dimensions={0} | all-to-all | bytes 458752 | tf_op jit(solution)/shard_map/all_to_all | solution.py:50
  163.7 5.2 %convolution_convert_fusion.3 = bf16[16,7168]{1,0:T(8,128)(2,1)S(1)} fusion(bf16[1,256,7168]{2,1,0:T(8,128)(2,1)} %param.19, bf16[16,7168]{1,0:T(8,128)(2,1)S(1)} %reshape.1047, bf16[1,7168,256]{2,1,0:T(8,128)(2,1)} %param.18, f32[16,256]{1,0:T(8,128)S(1)} %fusion.36), kind=kOutput, calls=%fused_computation.17 | convolution fusion | flops 117579776 | bytes 7815168 | tf_op jit(solution)/shard_map/dot_general | solution.py:55
  173.2 8.9 %all-to-all-done.7 = bf16[8,2,7168]{2,1,0:T(2,128)(2,1)S(1)} async-done(((bf16[8,2,7168]{2,1,0:T(2,128)(2,1)}), bf16[8,2,7168]{2,1,0:T(2,128)(2,1)S(1)}, u32[]{:S(2)}, u32[]{:S(2)}) %all-to-all-start.7) | async-done | bytes 229408 | tf_op jit(solution)/shard_map/all_to_all | solution.py:58
  183.0 5.2 %collective-permute-start.3 = (bf16[16,7168]{1,0:T(8,128)(2,1)S(1)}, bf16[16,7168]{1,0:T(8,128)(2,1)S(1)}, u32[]{:S(2)}, u32[]{:S(2)}) collective-permute-start(bf16[16,7168]{1,0:T(8,128)(2,1)S(1)} %fusion.3), channel_id=1, source_target_pairs={{0,8},{8,16},{16,24},{1,9},{9,17},{17,25},{2,10},{10,18},{18,26},{... | collective-permute-start | bytes 688136 | tf_op jit(solution)/shard_map/ppermute | solution.py:15
  188.2 4.5 %collective-permute-done.3 = bf16[16,7168]{1,0:T(8,128)(2,1)S(1)} collective-permute-done((bf16[16,7168]{1,0:T(8,128)(2,1)S(1)}, bf16[16,7168]{1,0:T(8,128)(2,1)S(1)}, u32[]{:S(2)}, u32[]{:S(2)}) %collective-permute-start.3) | collective-permute-done | bytes 229408 | tf_op jit(solution)/shard_map/ppermute | solution.py:15
  193.2 11.9 %all_to_all.79 = bf16[8,2,7168]{2,1,0:T(2,128)(2,1)S(1)} all-to-all(bf16[8,2,7168]{2,1,0:T(2,128)(2,1)S(1)} %reshape.1052), channel_id=1, replica_groups=mesh['section'=4,'expert'=8] {'expert'}, dimensions={0} | all-to-all | bytes 458752 | tf_op jit(solution)/shard_map/all_to_all | solution.py:50
  207.8 5.2 %convolution_convert_fusion.2 = bf16[16,7168]{1,0:T(8,128)(2,1)S(1)} fusion(bf16[1,256,7168]{2,1,0:T(8,128)(2,1)} %param.19, bf16[16,7168]{1,0:T(8,128)(2,1)S(1)} %reshape.1053, bf16[1,7168,256]{2,1,0:T(8,128)(2,1)} %param.18, f32[16,256]{1,0:T(8,128)S(1)} %fusion.34), kind=kOutput, calls=%fused_computation.16 | convolution fusion | flops 117579776 | bytes 7815168 | tf_op jit(solution)/shard_map/dot_general | solution.py:55
  217.4 8.9 %all-to-all-done.9 = bf16[8,2,7168]{2,1,0:T(2,128)(2,1)S(1)} async-done(((bf16[8,2,7168]{2,1,0:T(2,128)(2,1)}), bf16[8,2,7168]{2,1,0:T(2,128)(2,1)S(1)}, u32[]{:S(2)}, u32[]{:S(2)}) %all-to-all-start.9) | async-done | bytes 229408 | tf_op jit(solution)/shard_map/all_to_all | solution.py:58
  227.1 5.3 %collective-permute-start.4 = (bf16[16,7168]{1,0:T(8,128)(2,1)S(1)}, bf16[16,7168]{1,0:T(8,128)(2,1)S(1)}, u32[]{:S(2)}, u32[]{:S(2)}) collective-permute-start(bf16[16,7168]{1,0:T(8,128)(2,1)S(1)} %get-tuple-element.107), channel_id=1, source_target_pairs={{0,8},{8,16},{16,24},{1,9},{9,17},{17,25},{2,10},{10,18},{18,26},{... | collective-permute-start | bytes 688136 | tf_op jit(solution)/shard_map/ppermute | solution.py:15
  232.4 4.5 %collective-permute-done.4 = bf16[16,7168]{1,0:T(8,128)(2,1)S(1)} collective-permute-done((bf16[16,7168]{1,0:T(8,128)(2,1)S(1)}, bf16[16,7168]{1,0:T(8,128)(2,1)S(1)}, u32[]{:S(2)}, u32[]{:S(2)}) %collective-permute-start.4) | collective-permute-done | bytes 229408 | tf_op jit(solution)/shard_map/ppermute | solution.py:15
  237.5 11.9 %all_to_all.80 = bf16[8,2,7168]{2,1,0:T(2,128)(2,1)S(1)} all-to-all(bf16[8,2,7168]{2,1,0:T(2,128)(2,1)S(1)} %reshape.1058), channel_id=1, replica_groups=mesh['section'=4,'expert'=8] {'expert'}, dimensions={0} | all-to-all | bytes 458752 | tf_op jit(solution)/shard_map/all_to_all | solution.py:50
  252.1 5.2 %convolution_convert_fusion.1 = bf16[16,7168]{1,0:T(8,128)(2,1)S(1)} fusion(bf16[1,256,7168]{2,1,0:T(8,128)(2,1)} %param.19, bf16[16,7168]{1,0:T(8,128)(2,1)S(1)} %reshape.1059, bf16[1,7168,256]{2,1,0:T(8,128)(2,1)} %param.18, f32[16,256]{1,0:T(8,128)S(1)} %fusion.32), kind=kOutput, calls=%fused_computation.15 | convolution fusion | flops 117579776 | bytes 7815168 | tf_op jit(solution)/shard_map/dot_general | solution.py:55
  261.6 8.9 %all-to-all-done.11 = bf16[8,2,7168]{2,1,0:T(2,128)(2,1)S(1)} async-done(((bf16[8,2,7168]{2,1,0:T(2,128)(2,1)}), bf16[8,2,7168]{2,1,0:T(2,128)(2,1)S(1)}, u32[]{:S(2)}, u32[]{:S(2)}) %all-to-all-start.11) | async-done | bytes 229408 | tf_op jit(solution)/shard_map/all_to_all | solution.py:58
  271.3 5.3 %collective-permute-start.5 = (bf16[16,7168]{1,0:T(8,128)(2,1)S(1)}, bf16[16,7168]{1,0:T(8,128)(2,1)S(1)}, u32[]{:S(2)}, u32[]{:S(2)}) collective-permute-start(bf16[16,7168]{1,0:T(8,128)(2,1)S(1)} %get-tuple-element.109), channel_id=1, source_target_pairs={{0,8},{8,16},{16,24},{1,9},{9,17},{17,25},{2,10},{10,18},{18,26},{... | collective-permute-start | bytes 688136 | tf_op jit(solution)/shard_map/ppermute | solution.py:15
  276.6 4.5 %collective-permute-done.5 = bf16[16,7168]{1,0:T(8,128)(2,1)S(1)} collective-permute-done((bf16[16,7168]{1,0:T(8,128)(2,1)S(1)}, bf16[16,7168]{1,0:T(8,128)(2,1)S(1)}, u32[]{:S(2)}, u32[]{:S(2)}) %collective-permute-start.5) | collective-permute-done | bytes 229408 | tf_op jit(solution)/shard_map/ppermute | solution.py:15
  281.7 11.9 %all_to_all.81 = bf16[8,2,7168]{2,1,0:T(2,128)(2,1)S(1)} all-to-all(bf16[8,2,7168]{2,1,0:T(2,128)(2,1)S(1)} %reshape.1064), channel_id=1, replica_groups=mesh['section'=4,'expert'=8] {'expert'}, dimensions={0} | all-to-all | bytes 458752 | tf_op jit(solution)/shard_map/all_to_all | solution.py:50
  296.3 5.2 %convolution_convert_fusion = bf16[16,7168]{1,0:T(8,128)(2,1)S(1)} fusion(bf16[1,256,7168]{2,1,0:T(8,128)(2,1)} %param.19, bf16[16,7168]{1,0:T(8,128)(2,1)S(1)} %reshape.1065, bf16[1,7168,256]{2,1,0:T(8,128)(2,1)} %param.18, f32[16,256]{1,0:T(8,128)S(1)} %fusion.30), kind=kOutput, calls=%fused_computation.14 | convolution fusion | flops 117579776 | bytes 7815168 | tf_op jit(solution)/shard_map/dot_general | solution.py:55
  305.8 8.9 %all-to-all-done.13 = bf16[8,2,7168]{2,1,0:T(2,128)(2,1)S(1)} async-done(((bf16[8,2,7168]{2,1,0:T(2,128)(2,1)}), bf16[8,2,7168]{2,1,0:T(2,128)(2,1)S(1)}, u32[]{:S(2)}, u32[]{:S(2)}) %all-to-all-start.13) | async-done | bytes 229408 | tf_op jit(solution)/shard_map/all_to_all | solution.py:58
  315.5 18.8 %all_to_all.82 = bf16[4,16,7168]{2,1,0:T(8,128)(2,1)S(1)} all-to-all(bf16[4,16,7168]{2,1,0:T(8,128)(2,1)S(1)} %fusion.8), channel_id=1, replica_groups=mesh['section'=4,'expert'=8] {'section'}, dimensions={0} | all-to-all | bytes 1835008 | tf_op jit(solution)/shard_map/all_to_all | solution.py:105
  (128 shorter events, 75.2 us)
Async XLA Ops:
  35.6 10.7 %copy-start.1 = (f32[1,4,16,8]{2,3,1,0:T(8,128)S(1)}, f32[1,4,16,8]{2,3,1,0:T(8,128)}, u32[]{:S(2)}) copy-start(f32[1,4,16,8]{2,3,1,0:T(8,128)} %param.21) | copy-start | bytes 6148
  35.6 21.7 %copy-start = (s32[1,4,16,8]{2,3,1,0:T(8,128)S(1)}, s32[1,4,16,8]{2,3,1,0:T(8,128)}, u32[]{:S(2)}) copy-start(s32[1,4,16,8]{2,3,1,0:T(8,128)} %param.20) | copy-start | bytes 6148
  35.6 26.4 %copy-start.2 = (f32[1,7168]{1,0:T(1,128)S(1)}, f32[1,7168]{1,0:T(1,128)}, u32[]{:S(2)}) copy-start(f32[1,7168]{1,0:T(1,128)} %param.16) | copy-start | bytes 86020
  41.7 12.4 %all-to-all-start.1 = ((bf16[8,2,7168]{2,1,0:T(2,128)(2,1)}), bf16[8,2,7168]{2,1,0:T(2,128)(2,1)S(1)}, u32[]{:S(2)}, u32[]{:S(2)}) async-start(bf16[8,2,7168]{2,1,0:T(2,128)(2,1)} %reshape.1033), calls=%async_computation.1 | async-start | bytes 458752 | tf_op jit(solution)/shard_map/all_to_all | solution.py:58
  54.8 7.0 %collective-permute-start = (bf16[16,7168]{1,0:T(8,128)(2,1)S(1)}, bf16[16,7168]{1,0:T(8,128)(2,1)S(1)}, u32[]{:S(2)}, u32[]{:S(2)}) collective-permute-start(bf16[16,7168]{1,0:T(8,128)(2,1)S(1)} %fusion), channel_id=1, source_target_pairs={{0,8},{8,16},{16,24},{1,9},{9,17},{17,25},{2,10},{10,18},{18,26},{... | collective-permute-start | bytes 688136 | tf_op jit(solution)/shard_map/ppermute | solution.py:15
  83.0 12.4 %all-to-all-start.3 = ((bf16[8,2,7168]{2,1,0:T(2,128)(2,1)}), bf16[8,2,7168]{2,1,0:T(2,128)(2,1)S(1)}, u32[]{:S(2)}, u32[]{:S(2)}) async-start(bf16[8,2,7168]{2,1,0:T(2,128)(2,1)} %reshape.1038), calls=%async_computation.3 | async-start | bytes 458752 | tf_op jit(solution)/shard_map/all_to_all | solution.py:58
  96.2 8.9 %collective-permute-start.1 = (bf16[16,7168]{1,0:T(8,128)(2,1)S(1)}, bf16[16,7168]{1,0:T(8,128)(2,1)S(1)}, u32[]{:S(2)}, u32[]{:S(2)}) collective-permute-start(bf16[16,7168]{1,0:T(8,128)(2,1)S(1)} %fusion.1), channel_id=1, source_target_pairs={{0,8},{8,16},{16,24},{1,9},{9,17},{17,25},{2,10},{10,18},{18,26},{... | collective-permute-start | bytes 688136 | tf_op jit(solution)/shard_map/ppermute | solution.py:15
  126.4 12.4 %all-to-all-start.5 = ((bf16[8,2,7168]{2,1,0:T(2,128)(2,1)}), bf16[8,2,7168]{2,1,0:T(2,128)(2,1)S(1)}, u32[]{:S(2)}, u32[]{:S(2)}) async-start(bf16[8,2,7168]{2,1,0:T(2,128)(2,1)} %reshape.1043), calls=%async_computation.5 | async-start | bytes 458752 | tf_op jit(solution)/shard_map/all_to_all | solution.py:58
  139.6 8.9 %collective-permute-start.2 = (bf16[16,7168]{1,0:T(8,128)(2,1)S(1)}, bf16[16,7168]{1,0:T(8,128)(2,1)S(1)}, u32[]{:S(2)}, u32[]{:S(2)}) collective-permute-start(bf16[16,7168]{1,0:T(8,128)(2,1)S(1)} %fusion.2), channel_id=1, source_target_pairs={{0,8},{8,16},{16,24},{1,9},{9,17},{17,25},{2,10},{10,18},{18,26},{... | collective-permute-start | bytes 688136 | tf_op jit(solution)/shard_map/ppermute | solution.py:15
  169.8 12.4 %all-to-all-start.7 = ((bf16[8,2,7168]{2,1,0:T(2,128)(2,1)}), bf16[8,2,7168]{2,1,0:T(2,128)(2,1)S(1)}, u32[]{:S(2)}, u32[]{:S(2)}) async-start(bf16[8,2,7168]{2,1,0:T(2,128)(2,1)} %reshape.1048), calls=%async_computation.7 | async-start | bytes 458752 | tf_op jit(solution)/shard_map/all_to_all | solution.py:58
  183.0 9.7 %collective-permute-start.3 = (bf16[16,7168]{1,0:T(8,128)(2,1)S(1)}, bf16[16,7168]{1,0:T(8,128)(2,1)S(1)}, u32[]{:S(2)}, u32[]{:S(2)}) collective-permute-start(bf16[16,7168]{1,0:T(8,128)(2,1)S(1)} %fusion.3), channel_id=1, source_target_pairs={{0,8},{8,16},{16,24},{1,9},{9,17},{17,25},{2,10},{10,18},{18,26},{... | collective-permute-start | bytes 688136 | tf_op jit(solution)/shard_map/ppermute | solution.py:15
  213.9 12.4 %all-to-all-start.9 = ((bf16[8,2,7168]{2,1,0:T(2,128)(2,1)}), bf16[8,2,7168]{2,1,0:T(2,128)(2,1)S(1)}, u32[]{:S(2)}, u32[]{:S(2)}) async-start(bf16[8,2,7168]{2,1,0:T(2,128)(2,1)} %reshape.1054), calls=%async_computation.9 | async-start | bytes 458752 | tf_op jit(solution)/shard_map/all_to_all | solution.py:58
  227.1 9.8 %collective-permute-start.4 = (bf16[16,7168]{1,0:T(8,128)(2,1)S(1)}, bf16[16,7168]{1,0:T(8,128)(2,1)S(1)}, u32[]{:S(2)}, u32[]{:S(2)}) collective-permute-start(bf16[16,7168]{1,0:T(8,128)(2,1)S(1)} %get-tuple-element.107), channel_id=1, source_target_pairs={{0,8},{8,16},{16,24},{1,9},{9,17},{17,25},{2,10},{10,18},{18,26},{... | collective-permute-start | bytes 688136 | tf_op jit(solution)/shard_map/ppermute | solution.py:15
  258.1 12.4 %all-to-all-start.11 = ((bf16[8,2,7168]{2,1,0:T(2,128)(2,1)}), bf16[8,2,7168]{2,1,0:T(2,128)(2,1)S(1)}, u32[]{:S(2)}, u32[]{:S(2)}) async-start(bf16[8,2,7168]{2,1,0:T(2,128)(2,1)} %reshape.1060), calls=%async_computation.11 | async-start | bytes 458752 | tf_op jit(solution)/shard_map/all_to_all | solution.py:58
  271.3 9.8 %collective-permute-start.5 = (bf16[16,7168]{1,0:T(8,128)(2,1)S(1)}, bf16[16,7168]{1,0:T(8,128)(2,1)S(1)}, u32[]{:S(2)}, u32[]{:S(2)}) collective-permute-start(bf16[16,7168]{1,0:T(8,128)(2,1)S(1)} %get-tuple-element.109), channel_id=1, source_target_pairs={{0,8},{8,16},{16,24},{1,9},{9,17},{17,25},{2,10},{10,18},{18,26},{... | collective-permute-start | bytes 688136 | tf_op jit(solution)/shard_map/ppermute | solution.py:15
  302.4 12.4 %all-to-all-start.13 = ((bf16[8,2,7168]{2,1,0:T(2,128)(2,1)}), bf16[8,2,7168]{2,1,0:T(2,128)(2,1)S(1)}, u32[]{:S(2)}, u32[]{:S(2)}) async-start(bf16[8,2,7168]{2,1,0:T(2,128)(2,1)} %reshape.1066), calls=%async_computation.13 | async-start | bytes 458752 | tf_op jit(solution)/shard_map/all_to_all | solution.py:58
where the time goes:
time: 337 us; the launch traced here: 335 us
  blocking collectives  119 us (35%)
  waiting for transfers between devices  87.9 us (26%)
  matrix products  61.8 us (18%)
  starting transfers between devices  51 us (15%)
  local copies, waits for them, and re-layouts  8.44 us (3%)
  other arithmetic  6.67 us (2%)
    all_to_all x7, blocking collectives, moe_layer(): lax.all_to_all(send_all, 'expert', split_axis=0, concat_axis=0, tiled=True)  85.2 us
    all_to_all x7, waiting for transfers between devices, moe_layer(): lax.all_to_all(partial_value.reshape(n_dev, CAP, width_model), 'expert',...  61.2 us
    dot_general x7, matrix products, moe_layer(): jnp.dot(hidden, down_mat, preferred_element_type=jnp.float32)  36.7 us
    ppermute x6, starting transfers between devices, from_behind(): return lax.ppermute(array, axis, pairs)  27.2 us
    ppermute x6, waiting for transfers between devices, from_behind(): return lax.ppermute(array, axis, pairs)  26.7 us
    all_to_all x7, starting transfers between devices, moe_layer(): lax.all_to_all(partial_value.reshape(n_dev, CAP, width_model), 'expert',...  23.8 us
    all_to_all x1, blocking collectives, shards(): lax.all_to_all(finished, 'section', split_axis=0, concat_axis=0, tiled=True)  18.8 us
    dot_general x7, matrix products, moe_layer(): gate_val = jnp.dot(rows_in, gate_mat, preferred_element_type=jnp.float32)  18.4 us
  transfers between devices with their start and end apart: 13, of which 13 were waited for; matrix products, arithmetic and copies ran while one was open for 0% of the time, Pallas kernels for 0%

commit v1 on v0

v1 whole, which is shorter than its diff:
```python
import jax
import jax.numpy as jnp
from jax import lax
from jax.sharding import PartitionSpec as P

CAP = 2

eps_norm = 1e-06


def slot_weights(chosen, gates, num_experts):
    expert_range = jnp.arange(num_experts, dtype=jnp.int32)
    matched = (chosen[..., None] == expert_range).astype(jnp.int32)
    hit_table = jnp.sum(matched, axis=-2, dtype=jnp.int32)
    tokens = chosen.shape[-2]
    before = jnp.arange(tokens)[:, None] > jnp.arange(tokens)[None, :]
    earlier = jnp.sum(
        jnp.where(before[:, :, None], hit_table[..., None, :, :], 0), axis=-2, dtype=jnp.int32
    )
    weight = jnp.sum(jnp.where(matched > 0, gates[..., None], 0.0), axis=-2)
    slots = jnp.arange(CAP, dtype=jnp.int32)
    table = jnp.where(earlier[..., None] == slots, weight[..., None], 0.0)
    return table.reshape(table.shape[:-2] + (num_experts * CAP,))


def swap(array, axis, by):
    devices = lax.axis_size(axis)
    return lax.ppermute(array, axis, [(i, i ^ by) for i in range(devices)])


def section_exchange(parts):
    return [parts[0]] + [swap(parts[k], "section", k) for k in range(1, len(parts))]


def dispatch(rows):
    experts, count, width = rows.shape
    n_dev = lax.axis_size("expert")
    if n_dev == 8:
        own = rows[0]
        near = jnp.stack([own] + [swap(own, "expert", 2 * k) for k in range(1, 4)])
        return jnp.concatenate([near, swap(near, "expert", 1)])
    send = jnp.repeat(rows, n_dev // experts, axis=0)
    return lax.all_to_all(send, "expert", split_axis=0, concat_axis=0, tiled=True)


def collect(partial, experts):
    n_dev, count, width = partial.shape
    if n_dev == 8:
        other = swap(partial[4:], "expert", 1)
        both = (partial[:4].astype(jnp.float32) + other.astype(jnp.float32)).astype(jnp.bfloat16)
        got = [both[0]] + [swap(both[k], "expert", 2 * k) for k in range(1, 4)]
        return sum(g.astype(jnp.float32) for g in got)[None]
    back = lax.all_to_all(partial, "expert", split_axis=0, concat_axis=0, tiled=True)
    back = back.reshape(experts, n_dev // experts, count, width)
    return jnp.sum(back.astype(jnp.float32), axis=1)


def expert_block(rows_in, gate_mat, up_mat, down_mat):
    gate_val = jnp.dot(rows_in, gate_mat, preferred_element_type=jnp.float32)
    up_val = jnp.dot(rows_in, up_mat, preferred_element_type=jnp.float32)
    hidden = (jax.nn.silu(gate_val) * up_val).astype(jnp.bfloat16)
    return jnp.dot(hidden, down_mat, preferred_element_type=jnp.float32).astype(jnp.bfloat16)


def layer_round(sent, gain_row, gate_mat, up_mat, down_mat, num_experts):
    width = sent[0].shape[-1]
    here = jnp.stack(section_exchange(sent))
    rows_float = here.astype(jnp.float32)
    scale = lax.rsqrt(jnp.mean(rows_float * rows_float, axis=-1, keepdims=True) + eps_norm)
    normed = (rows_float * scale * gain_row).astype(jnp.bfloat16)
    micros = here.shape[0]
    normed = normed.reshape(micros, num_experts, CAP, width).transpose(1, 0, 2, 3)
    received = dispatch(normed.reshape(num_experts, micros * CAP, width))
    n_dev = received.shape[0]
    partial = expert_block(received.reshape(-1, width), gate_mat, up_mat, down_mat)
    total = collect(partial.reshape(n_dev, micros * CAP, width), num_experts)
    total = total.astype(jnp.bfloat16).reshape(num_experts, micros, CAP, width)
    total = total.transpose(1, 0, 2, 3).reshape(micros, num_experts * CAP, width)
    return section_exchange([total[k] for k in range(micros)])


def shards(embedded, norm_gain, gate_proj, up_proj, down_proj, expert_ids, route_gates):
    n_section = lax.axis_size("section")
    n_dev = lax.axis_size("expert")
    num_experts = n_dev // min(8, n_dev)
    me = lax.axis_index("section")
    base = embedded[0]
    own = slot_weights(expert_ids[0], route_gates[0], num_experts)

    def pick(stacked, index):
        return lax.dynamic_index_in_dim(stacked, index, 0, keepdims=False)

    tables = section_exchange([pick(own, me ^ k) for k in range(n_section)])
    tables = jnp.stack(tables)
    ordered = jnp.stack([pick(tables, me ^ l) for l in range(n_section)])
    chosen = ordered > 0
    picks = jnp.sum(jnp.any(chosen, axis=-1).astype(jnp.int32), axis=0)
    depth = lax.pmax(jnp.max(picks), ("section", "expert"))
    masks = chosen.astype(jnp.bfloat16)

    def take(mask, rows):
        return lax.dot_general(
            mask, rows, (((0,), (0,)), ((), ())), preferred_element_type=jnp.float32
        ).astype(jnp.bfloat16)

    def advance(rows, layer, update):
        routed = jnp.dot(
            ordered[layer],
            update.astype(jnp.float32),
            precision=lax.Precision.HIGHEST,
            preferred_element_type=jnp.float32,
        )
        return (rows.astype(jnp.float32) + routed).astype(jnp.bfloat16)

    def one_round(inputs):
        sent = [pick(inputs, me ^ k) for k in range(n_section)]
        got = jnp.stack(
            layer_round(sent, norm_gain[0], gate_proj[0], up_proj[0], down_proj[0], num_experts)
        )
        return jnp.stack([pick(got, me ^ l) for l in range(n_section)])

    def body(state):
        count, updates = state
        rows, inputs = base, []
        for layer in range(n_section):
            inputs.append(take(masks[layer], rows))
            if layer < n_section - 1:
                rows = advance(rows, layer, updates[layer])
        return count + 1, one_round(jnp.stack(inputs))

    first = jnp.stack([take(masks[layer], base) for layer in range(n_section)])
    updates = one_round(first)
    _, updates = lax.while_loop(lambda s: s[0] < depth, body, (jnp.int32(1), updates))
    rows = base
    for layer in range(n_section):
        rows = advance(rows, layer, updates[layer])
    return rows[None]


def solution(mesh):
    placed = (
        P("section", "expert", None),
        P("section", None),
        P("section", None, "expert"),
        P("section", None, "expert"),
        P("section", "expert", None),
        P("section", None, "expert", None),
        P("section", None, "expert", None),
    )
    return jax.shard_map(
        shards, mesh=mesh, in_specs=placed, out_specs=P("section", "expert", None), check_vma=False
    )
```

time: 337 us -> 159 us (0.47)
  blocking collectives: 119 us -> 39 us
  waiting for transfers between devices: 87.9 us -> 47.1 us
  matrix products: 61.8 us -> 25.1 us
  starting transfers between devices: 51 us -> 37.1 us
  local copies, waits for them, and re-layouts: 8.44 us -> 1.61 us
    all_to_all x8 -> x0, blocking collectives: 104 us -> none  [the longest x7 85.2 us: moe_layer(): lax.all_to_all(send_all, 'expert', split_axis=0, concat_axis=0, tiled=True)]
    all_to_all x7 -> x0, waiting for transfers between devices: 61.2 us -> none  [moe_layer(): lax.all_to_all(partial_value.reshape(n_dev, CAP, width_model), 'expert',...]
    pmax x0 -> x1, blocking collectives: none -> 39 us  [shards(): depth = lax.pmax(jnp.max(picks), ('section', 'expert'))]
    dot_general x28 -> x18, matrix products: 61.8 us -> 25.1 us  [the longest x2 10.9 us: expert_block(): jnp.dot(hidden, down_mat, preferred_element_type=jnp.float32)]
    all_to_all x7 -> x0, starting transfers between devices: 23.8 us -> none  [moe_layer(): lax.all_to_all(partial_value.reshape(n_dev, CAP, width_model), 'expert',...]
    ppermute x6 -> x31, waiting for transfers between devices: 26.7 us -> 47.1 us  [swap(): return lax.ppermute(array, axis, [(i, i ^ by) for i in range(devices)])]
    all_gather x1 -> x0, blocking collectives: 14.9 us -> none  [shards(): every_block = lax.all_gather(embedded, 'section', axis=0, tiled=True)]
    ppermute x6 -> x31, starting transfers between devices: 27.2 us -> 37.1 us  [swap(): return lax.ppermute(array, axis, [(i, i ^ by) for i in range(devices)])]
  transfers between devices with their start and end apart: 13 -> 31, of which waited for: 13 -> 25; matrix products, arithmetic and copies ran while one was open for 0% -> 1% of each run, Pallas kernels for 0% -> 0%
where the time goes in v1:
time: 159 us; the launch traced here: 158 us
  waiting for transfers between devices  47.1 us (30%)
  blocking collectives  39 us (25%)
  starting transfers between devices  37.1 us (23%)
  matrix products  25.1 us (16%)
  other arithmetic  6.53 us (4%)
  loops' own time  1.78 us (1%)
  local copies, waits for them, and re-layouts  1.61 us (1%)
    ppermute x31, waiting for transfers between devices, swap(): return lax.ppermute(array, axis, [(i, i ^ by) for i in range(devices)])  47.1 us
    pmax x1, blocking collectives, shards(): depth = lax.pmax(jnp.max(picks), ('section', 'expert'))  39 us
    ppermute x31, starting transfers between devices, swap(): return lax.ppermute(array, axis, [(i, i ^ by) for i in range(devices)])  37.1 us
    dot_general x2, matrix products, expert_block(): jnp.dot(hidden, down_mat, preferred_element_type=jnp.float32)  10.9 us
    dot_general x2, matrix products, expert_block(): up_val = jnp.dot(rows_in, up_mat, preferred_element_type=jnp.float32)  5.5 us
    dot_general x7, matrix products, take(): lax.dot_general(mask, rows, (((0,), (0,)), ((), ())), preferred_element_t...  4.86 us
    dot_general x7, matrix products, advance(): jnp.dot(ordered[layer], update.astype(jnp.float32), precision=lax.Precisi...  3.78 us
  transfers between devices with their start and end apart: 31, of which 25 were waited for; matrix products, arithmetic and copies ran while one was open for 1% of the time, Pallas kernels for 0%

profile of v1, /device:TPU:0, one launch (start us, length us, event | category | flops | bytes accessed | tf_op | source)
XLA Modules:
  0.0 158.5 jit_solution(4030403617276192796)
XLA Ops:
  1.7 4.0 %collective-permute-start.16 = (f32[16,2]{0,1:T(2,128)S(1)}, f32[16,2]{0,1:T(2,128)S(1)}, u32[]{:S(2)}, u32[]{:S(2)}) collective-permute-start(f32[16,2]{0,1:T(2,128)S(1)} %get-tuple-element.273), channel_id=1, source_target_pairs={{0,24},{8,16},{16,8},{24,0},{1,25},{9,17},{17,9},{25,1},{2,26},{10... | collective-permute-start | bytes 392 | tf_op jit(solution)/shard_map/ppermute | solution.py:28
  7.2 2.0 %collective-permute-done.15 = f32[16,2]{0,1:T(2,128)S(1)} collective-permute-done((f32[16,2]{0,1:T(2,128)S(1)}, f32[16,2]{0,1:T(2,128)S(1)}, u32[]{:S(2)}, u32[]{:S(2)}) %collective-permute-start.15) | collective-permute-done | bytes 160 | tf_op jit(solution)/shard_map/ppermute | solution.py:28
  16.2 1.9 %collective-permute-start.17 = (bf16[2,7168]{1,0:T(2,128)(2,1)S(1)}, bf16[2,7168]{1,0:T(2,128)(2,1)S(1)}, u32[]{:S(2)}, u32[]{:S(2)}) collective-permute-start(bf16[2,7168]{1,0:T(2,128)(2,1)S(1)} %get-tuple-element.267), channel_id=1, source_target_pairs={{0,8},{8,0},{16,24},{24,16},{1,9},{9,1},{17,25},{25,17},{2,10},{10... | collective-permute-start | bytes 86024 | tf_op jit(solution)/shard_map/ppermute | solution.py:28
  21.6 4.1 %collective-permute-start.22 = (bf16[8,7168]{1,0:T(8,128)(2,1)S(1)}, bf16[8,7168]{1,0:T(8,128)(2,1)S(1)}, u32[]{:S(2)}, u32[]{:S(2)}) collective-permute-start(bf16[8,7168]{1,0:T(8,128)(2,1)S(1)} %multiply_convert_fusion.4), channel_id=1, source_target_pairs={{0,6},{1,7},{2,4},{3,5},{4,2},{5,3},{6,0},{7,1},{8,14},{9,15},{10,... | collective-permute-start | bytes 344072 | tf_op jit(solution)/shard_map/ppermute | solution.py:28
  27.1 1.8 %collective-permute-done.22 = bf16[8,7168]{1,0:T(8,128)(2,1)S(1)} collective-permute-done((bf16[8,7168]{1,0:T(8,128)(2,1)S(1)}, bf16[8,7168]{1,0:T(8,128)(2,1)S(1)}, u32[]{:S(2)}, u32[]{:S(2)}) %collective-permute-start.22) | collective-permute-done | bytes 114720 | tf_op jit(solution)/shard_map/ppermute | solution.py:28
  29.0 2.9 %collective-permute-done.21 = bf16[8,7168]{1,0:T(8,128)(2,1)S(1)} collective-permute-done((bf16[8,7168]{1,0:T(8,128)(2,1)S(1)}, bf16[8,7168]{1,0:T(8,128)(2,1)S(1)}, u32[]{:S(2)}, u32[]{:S(2)}) %collective-permute-start.21) | collective-permute-done | bytes 114720 | tf_op jit(solution)/shard_map/ppermute | solution.py:28
  32.1 1.7 %collective-permute-done.23 = bf16[4,8,7168]{2,1,0:T(8,128)(2,1)S(1)} collective-permute-done((bf16[4,8,7168]{2,1,0:T(8,128)(2,1)S(1)}, bf16[4,8,7168]{2,1,0:T(8,128)(2,1)S(1)}, u32[]{:S(2)}, u32[]{:S(2)}) %collective-permute-start.23) | collective-permute-done | bytes 458784 | tf_op jit(solution)/shard_map/ppermute | solution.py:28
  33.9 2.8 %fusion.52 = f32[64,256]{1,0:T(8,128)S(1)} fusion(bf16[1,7168,256]{2,1,0:T(8,128)(2,1)} %param.12, bf16[8,8,7168]{2,1,0:T(8,128)(2,1)S(1)} %constant_dynamic-update-slice_fusion.5), kind=kOutput, calls=%fused_computation.94 | convolution fusion | flops 234881024 | bytes 4653056 | tf_op jit(solution)/shard_map/dot_general | solution.py:60
  36.6 5.5 %convolution_convert_fusion.4 = bf16[64,7168]{1,0:T(8,128)(2,1)S(1)} fusion(bf16[1,256,7168]{2,1,0:T(8,128)(2,1)} %param.13, f32[64,256]{1,0:T(8,128)S(1)} %fusion.52, bf16[1,7168,256]{2,1,0:T(8,128)(2,1)} %param.11, bf16[8,8,7168]{2,1,0:T(8,128)(2,1)S(1)} %constant_dynamic-update-slice_fusion.5), kind=kOutput, calls=%fused_computation.73 | convolution fusion | flops 470319104 | bytes 9240576 | tf_op jit(solution)/shard_map/dot_general | solution.py:62
  42.4 1.7 %collective-permute-done.24 = bf16[4,8,7168]{2,1,0:T(8,128)(2,1)S(1)} collective-permute-done((bf16[4,8,7168]{2,1,0:T(8,128)(2,1)S(1)}, bf16[4,8,7168]{2,1,0:T(8,128)(2,1)S(1)}, u32[]{:S(2)}, u32[]{:S(2)}) %collective-permute-start.24) | collective-permute-done | bytes 458784 | tf_op jit(solution)/shard_map/ppermute | solution.py:28
  45.3 1.9 %collective-permute-start.27 = (bf16[8,7168]{1,0:T(8,128)(2,1)S(1)}, bf16[8,7168]{1,0:T(8,128)(2,1)S(1)}, u32[]{:S(2)}, u32[]{:S(2)}) collective-permute-start(bf16[8,7168]{1,0:T(8,128)(2,1)S(1)} %get-tuple-element.254), channel_id=1, source_target_pairs={{0,6},{1,7},{2,4},{3,5},{4,2},{5,3},{6,0},{7,1},{8,14},{9,15},{10,... | collective-permute-start | bytes 344072 | tf_op jit(solution)/shard_map/ppermute | solution.py:28
  47.8 1.7 %collective-permute-done.25 = bf16[8,7168]{1,0:T(8,128)(2,1)S(1)} collective-permute-done((bf16[8,7168]{1,0:T(8,128)(2,1)S(1)}, bf16[8,7168]{1,0:T(8,128)(2,1)S(1)}, u32[]{:S(2)}, u32[]{:S(2)}) %collective-permute-start.25) | collective-permute-done | bytes 114720 | tf_op jit(solution)/shard_map/ppermute | solution.py:28
  49.5 4.2 %collective-permute-done.27 = bf16[8,7168]{1,0:T(8,128)(2,1)S(1)} collective-permute-done((bf16[8,7168]{1,0:T(8,128)(2,1)S(1)}, bf16[8,7168]{1,0:T(8,128)(2,1)S(1)}, u32[]{:S(2)}, u32[]{:S(2)}) %collective-permute-start.27) | collective-permute-done | bytes 114720 | tf_op jit(solution)/shard_map/ppermute | solution.py:28
  53.6 4.4 %collective-permute-done.26 = bf16[8,7168]{1,0:T(8,128)(2,1)S(1)} collective-permute-done((bf16[8,7168]{1,0:T(8,128)(2,1)S(1)}, bf16[8,7168]{1,0:T(8,128)(2,1)S(1)}, u32[]{:S(2)}, u32[]{:S(2)}) %collective-permute-start.26) | collective-permute-done | bytes 114720 | tf_op jit(solution)/shard_map/ppermute | solution.py:28
  58.2 2.5 %collective-permute-start.30 = (bf16[2,7168]{1,0:T(2,128)(2,1)S(1)}, bf16[2,7168]{1,0:T(2,128)(2,1)S(1)}, u32[]{:S(2)}, u32[]{:S(2)}) collective-permute-start(bf16[2,7168]{1,0:T(2,128)(2,1)S(1)} %get-tuple-element.261), channel_id=1, source_target_pairs={{0,24},{8,16},{16,8},{24,0},{1,25},{9,17},{17,9},{25,1},{2,26},{10... | collective-permute-start | bytes 86024 | tf_op jit(solution)/shard_map/ppermute | solution.py:28
  62.5 39.0 %pmax.7 = s32[]{:T(128)} all-reduce(s32[]{:T(128)} %reduce_max.9), channel_id=1, replica_groups=mesh['section'=4,'expert'=8] {'section','expert'}, use_global_device_ids=true, to_apply=%region_7.8 | all-reduce | flops 1 | bytes 8 | tf_op jit(solution)/shard_map/pmax | solution.py:98
  102.1 53.9 %while.12 = (s32[]{:T(128)}, bf16[4,2,7168]{2,1,0:T(2,128)(2,1)S(1)}, s32[]{:T(128)}, bf16[2,7168]{1,0:T(2,128)(2,1)S(1)}, bf16[16,7168]{1,0:T(8,128)(2,1)S(1)},...) while((s32[]{:T(128)}, ...), condition=%wide.region_10.11_spmd, body=%wide.region_8.10_spmd.sunk | while | flops 719177728 | bytes 32822740 | solution.py:133
  105.1 2.6 %collective-permute-start = (bf16[2,7168]{1,0:T(2,128)(2,1)S(1)}, bf16[2,7168]{1,0:T(2,128)(2,1)S(1)}, u32[]{:S(2)}, u32[]{:S(2)}) collective-permute-start(bf16[2,7168]{1,0:T(2,128)(2,1)S(1)} %get-tuple-element.399), channel_id=1, source_target_pairs={{0,24},{8,16},{16,8},{24,0},{1,25},{9,17},{17,9},{25,1},{2,26},{10... | collective-permute-start | bytes 86024 | tf_op jit(solution)/shard_map/while/body/ppermute | solution.py:28
  109.9 1.6 %collective-permute-done.1 = bf16[2,7168]{1,0:T(2,128)(2,1)S(1)} collective-permute-done((bf16[2,7168]{1,0:T(2,128)(2,1)S(1)}, bf16[2,7168]{1,0:T(2,128)(2,1)S(1)}, u32[]{:S(2)}, u32[]{:S(2)}) %collective-permute-start.1) | collective-permute-done | bytes 28704 | tf_op jit(solution)/shard_map/while/body/ppermute | solution.py:28
  113.6 1.6 %collective-permute-start.5 = (bf16[8,7168]{1,0:T(8,128)(2,1)S(1)}, bf16[8,7168]{1,0:T(8,128)(2,1)S(1)}, u32[]{:S(2)}, u32[]{:S(2)}) collective-permute-start(bf16[8,7168]{1,0:T(8,128)(2,1)S(1)} %multiply_convert_fusion.13), channel_id=1, source_target_pairs={{0,6},{1,7},{2,4},{3,5},{4,2},{5,3},{6,0},{7,1},{8,14},{9,15},{10,... | collective-permute-start | bytes 344072 | tf_op jit(solution)/shard_map/while/body/ppermute | solution.py:28
  115.2 2.1 %collective-permute-start.4 = (bf16[8,7168]{1,0:T(8,128)(2,1)S(1)}, bf16[8,7168]{1,0:T(8,128)(2,1)S(1)}, u32[]{:S(2)}, u32[]{:S(2)}) collective-permute-start(bf16[8,7168]{1,0:T(8,128)(2,1)S(1)} %multiply_convert_fusion.13), channel_id=1, source_target_pairs={{0,4},{1,5},{2,6},{3,7},{4,0},{5,1},{6,2},{7,3},{8,12},{9,13},{10,... | collective-permute-start | bytes 344072 | tf_op jit(solution)/shard_map/while/body/ppermute | solution.py:28
  118.1 2.4 %collective-permute-done.5 = bf16[8,7168]{1,0:T(8,128)(2,1)S(1)} collective-permute-done((bf16[8,7168]{1,0:T(8,128)(2,1)S(1)}, bf16[8,7168]{1,0:T(8,128)(2,1)S(1)}, u32[]{:S(2)}, u32[]{:S(2)}) %collective-permute-start.5) | collective-permute-done | bytes 114720 | tf_op jit(solution)/shard_map/while/body/ppermute | solution.py:28
  120.5 4.0 %collective-permute-done.4 = bf16[8,7168]{1,0:T(8,128)(2,1)S(1)} collective-permute-done((bf16[8,7168]{1,0:T(8,128)(2,1)S(1)}, bf16[8,7168]{1,0:T(8,128)(2,1)S(1)}, u32[]{:S(2)}, u32[]{:S(2)}) %collective-permute-start.4) | collective-permute-done | bytes 114720 | tf_op jit(solution)/shard_map/while/body/ppermute | solution.py:28
  124.8 1.7 %collective-permute-done.6 = bf16[4,8,7168]{2,1,0:T(8,128)(2,1)S(1)} collective-permute-done((bf16[4,8,7168]{2,1,0:T(8,128)(2,1)S(1)}, bf16[4,8,7168]{2,1,0:T(8,128)(2,1)S(1)}, u32[]{:S(2)}, u32[]{:S(2)}) %collective-permute-start.6) | collective-permute-done | bytes 458784 | tf_op jit(solution)/shard_map/while/body/ppermute | solution.py:28
  126.6 2.8 %fusion.152 = f32[64,256]{1,0:T(8,128)S(1)} fusion(bf16[1,7168,256]{2,1,0:T(8,128)(2,1)} %get-tuple-element.469, bf16[8,8,7168]{2,1,0:T(8,128)(2,1)S(1)} %constant_dynamic-update-slice_fusion.19), kind=kOutput, calls=%fused_computation.14.clone.1 | convolution fusion | flops 234881024 | bytes 4653056 | tf_op jit(solution)/shard_map/while/body/dot_general | solution.py:60
  129.3 5.5 %convolution_convert_fusion.10 = bf16[64,7168]{1,0:T(8,128)(2,1)S(1)} fusion(bf16[1,256,7168]{2,1,0:T(8,128)(2,1)} %get-tuple-element.470, f32[64,256]{1,0:T(8,128)S(1)} %fusion.152, bf16[1,7168,256]{2,1,0:T(8,128)(2,1)} %get-tuple-element.468, bf16[8,8,7168]{2,1,0:T(8,128)(2,1)S(1)} %constant_dynamic-update-slice_fusion.19), kind=kOutput, calls=%fused_computation.clone.1 | convolution fusion | flops 470319104 | bytes 9240576 | tf_op jit(solution)/shard_map/while/body/dot_general | solution.py:62
  135.0 1.7 %collective-permute-done.7 = bf16[4,8,7168]{2,1,0:T(8,128)(2,1)S(1)} collective-permute-done((bf16[4,8,7168]{2,1,0:T(8,128)(2,1)S(1)}, bf16[4,8,7168]{2,1,0:T(8,128)(2,1)S(1)}, u32[]{:S(2)}, u32[]{:S(2)}) %collective-permute-start.7) | collective-permute-done | bytes 458784 | tf_op jit(solution)/shard_map/while/body/ppermute | solution.py:28
  136.8 1.8 %collective-permute-start.8 = (bf16[8,7168]{1,0:T(8,128)(2,1)S(1)}, bf16[8,7168]{1,0:T(8,128)(2,1)S(1)}, u32[]{:S(2)}, u32[]{:S(2)}) collective-permute-start(bf16[8,7168]{1,0:T(8,128)(2,1)S(1)} %get-tuple-element.407), channel_id=1, source_target_pairs={{0,6},{1,7},{2,4},{3,5},{4,2},{5,3},{6,0},{7,1},{8,14},{9,15},{10,... | collective-permute-start | bytes 344072 | tf_op jit(solution)/shard_map/while/body/ppermute | solution.py:28
  138.7 2.6 %collective-permute-start.10 = (bf16[8,7168]{1,0:T(8,128)(2,1)S(1)}, bf16[8,7168]{1,0:T(8,128)(2,1)S(1)}, u32[]{:S(2)}, u32[]{:S(2)}) collective-permute-start(bf16[8,7168]{1,0:T(8,128)(2,1)S(1)} %get-tuple-element.409), channel_id=1, source_target_pairs={{0,2},{1,3},{2,0},{3,1},{4,6},{5,7},{6,4},{7,5},{8,10},{9,11},{10,... | collective-permute-start | bytes 344072 | tf_op jit(solution)/shard_map/while/body/ppermute | solution.py:28
  141.3 3.5 %collective-permute-done.8 = bf16[8,7168]{1,0:T(8,128)(2,1)S(1)} collective-permute-done((bf16[8,7168]{1,0:T(8,128)(2,1)S(1)}, bf16[8,7168]{1,0:T(8,128)(2,1)S(1)}, u32[]{:S(2)}, u32[]{:S(2)}) %collective-permute-start.8) | collective-permute-done | bytes 114720 | tf_op jit(solution)/shard_map/while/body/ppermute | solution.py:28
  144.8 4.0 %collective-permute-done.9 = bf16[8,7168]{1,0:T(8,128)(2,1)S(1)} collective-permute-done((bf16[8,7168]{1,0:T(8,128)(2,1)S(1)}, bf16[8,7168]{1,0:T(8,128)(2,1)S(1)}, u32[]{:S(2)}, u32[]{:S(2)}) %collective-permute-start.9) | collective-permute-done | bytes 114720 | tf_op jit(solution)/shard_map/while/body/ppermute | solution.py:28
  150.9 1.6 %collective-permute-start.13 = (bf16[2,7168]{1,0:T(2,128)(2,1)S(1)}, bf16[2,7168]{1,0:T(2,128)(2,1)S(1)}, u32[]{:S(2)}, u32[]{:S(2)}) collective-permute-start(bf16[2,7168]{1,0:T(2,128)(2,1)S(1)} %get-tuple-element.412), channel_id=1, source_target_pairs={{0,8},{8,0},{16,24},{24,16},{1,9},{9,1},{17,25},{25,17},{2,10},{10... | collective-permute-start | bytes 86024 | tf_op jit(solution)/shard_map/while/body/ppermute | solution.py:28
  (110 shorter events, 34.9 us)
Async XLA Ops:
  1.7 5.5 %collective-permute-start.16 = (f32[16,2]{0,1:T(2,128)S(1)}, f32[16,2]{0,1:T(2,128)S(1)}, u32[]{:S(2)}, u32[]{:S(2)}) collective-permute-start(f32[16,2]{0,1:T(2,128)S(1)} %get-tuple-element.273), channel_id=1, source_target_pairs={{0,24},{8,16},{16,8},{24,0},{1,25},{9,17},{17,9},{25,1},{2,26},{10... | collective-permute-start | bytes 392 | tf_op jit(solution)/shard_map/ppermute | solution.py:28
  5.6 3.6 %collective-permute-start.15 = (f32[16,2]{0,1:T(2,128)S(1)}, f32[16,2]{0,1:T(2,128)S(1)}, u32[]{:S(2)}, u32[]{:S(2)}) collective-permute-start(f32[16,2]{0,1:T(2,128)S(1)} %get-tuple-element.274), channel_id=1, source_target_pairs={{0,16},{8,24},{16,0},{24,8},{1,17},{9,25},{17,1},{25,9},{2,18},{10... | collective-permute-start | bytes 392 | tf_op jit(solution)/shard_map/ppermute | solution.py:28
  6.2 3.6 %collective-permute-start.14 = (f32[16,2]{0,1:T(2,128)S(1)}, f32[16,2]{0,1:T(2,128)S(1)}, u32[]{:S(2)}, u32[]{:S(2)}) collective-permute-start(f32[16,2]{0,1:T(2,128)S(1)} %get-tuple-element.275), channel_id=1, source_target_pairs={{0,8},{8,0},{16,24},{24,16},{1,9},{9,1},{17,25},{25,17},{2,10},{10... | collective-permute-start | bytes 392 | tf_op jit(solution)/shard_map/ppermute | solution.py:28
  14.5 4.8 %collective-permute-start.19 = (bf16[2,7168]{1,0:T(2,128)(2,1)S(1)}, bf16[2,7168]{1,0:T(2,128)(2,1)S(1)}, u32[]{:S(2)}, u32[]{:S(2)}) collective-permute-start(bf16[2,7168]{1,0:T(2,128)(2,1)S(1)} %get-tuple-element.265), channel_id=1, source_target_pairs={{0,24},{8,16},{16,8},{24,0},{1,25},{9,17},{17,9},{25,1},{2,26},{10... | collective-permute-start | bytes 86024 | tf_op jit(solution)/shard_map/ppermute | solution.py:28
  16.0 3.9 %collective-permute-start.18 = (bf16[2,7168]{1,0:T(2,128)(2,1)S(1)}, bf16[2,7168]{1,0:T(2,128)(2,1)S(1)}, u32[]{:S(2)}, u32[]{:S(2)}) collective-permute-start(bf16[2,7168]{1,0:T(2,128)(2,1)S(1)} %get-tuple-element.266), channel_id=1, source_target_pairs={{0,16},{8,24},{16,0},{24,8},{1,17},{9,25},{17,1},{25,9},{2,18},{10... | collective-permute-start | bytes 86024 | tf_op jit(solution)/shard_map/ppermute | solution.py:28
  16.2 3.9 %collective-permute-start.17 = (bf16[2,7168]{1,0:T(2,128)(2,1)S(1)}, bf16[2,7168]{1,0:T(2,128)(2,1)S(1)}, u32[]{:S(2)}, u32[]{:S(2)}) collective-permute-start(bf16[2,7168]{1,0:T(2,128)(2,1)S(1)} %get-tuple-element.267), channel_id=1, source_target_pairs={{0,8},{8,0},{16,24},{24,16},{1,9},{9,1},{17,25},{25,17},{2,10},{10... | collective-permute-start | bytes 86024 | tf_op jit(solution)/shard_map/ppermute | solution.py:28
  21.6 7.4 %collective-permute-start.22 = (bf16[8,7168]{1,0:T(8,128)(2,1)S(1)}, bf16[8,7168]{1,0:T(8,128)(2,1)S(1)}, u32[]{:S(2)}, u32[]{:S(2)}) collective-permute-start(bf16[8,7168]{1,0:T(8,128)(2,1)S(1)} %multiply_convert_fusion.4), channel_id=1, source_target_pairs={{0,6},{1,7},{2,4},{3,5},{4,2},{5,3},{6,0},{7,1},{8,14},{9,15},{10,... | collective-permute-start | bytes 344072 | tf_op jit(solution)/shard_map/ppermute | solution.py:28
  25.6 6.2 %collective-permute-start.21 = (bf16[8,7168]{1,0:T(8,128)(2,1)S(1)}, bf16[8,7168]{1,0:T(8,128)(2,1)S(1)}, u32[]{:S(2)}, u32[]{:S(2)}) collective-permute-start(bf16[8,7168]{1,0:T(8,128)(2,1)S(1)} %multiply_convert_fusion.4), channel_id=1, source_target_pairs={{0,4},{1,5},{2,6},{3,7},{4,0},{5,1},{6,2},{7,3},{8,12},{9,13},{10,... | collective-permute-start | bytes 344072 | tf_op jit(solution)/shard_map/ppermute | solution.py:28
  25.6 6.2 %collective-permute-start.20 = (bf16[8,7168]{1,0:T(8,128)(2,1)S(1)}, bf16[8,7168]{1,0:T(8,128)(2,1)S(1)}, u32[]{:S(2)}, u32[]{:S(2)}) collective-permute-start(bf16[8,7168]{1,0:T(8,128)(2,1)S(1)} %multiply_convert_fusion.4), channel_id=1, source_target_pairs={{0,2},{1,3},{2,0},{3,1},{4,6},{5,7},{6,4},{7,5},{8,10},{9,11},{10,... | collective-permute-start | bytes 344072 | tf_op jit(solution)/shard_map/ppermute | solution.py:28
  32.0 1.9 %collective-permute-start.23 = (bf16[4,8,7168]{2,1,0:T(8,128)(2,1)S(1)}, bf16[4,8,7168]{2,1,0:T(8,128)(2,1)S(1)}, u32[]{:S(2)}, u32[]{:S(2)}) collective-permute-start(bf16[4,8,7168]{2,1,0:T(8,128)(2,1)S(1)} %pad_maximum_fusion.4), channel_id=1, source_target_pairs={{0,1},{1,0},{2,3},{3,2},{4,5},{5,4},{6,7},{7,6},{8,9},{9,8},{10,11... | collective-permute-start | bytes 1376264 | tf_op jit(solution)/shard_map/ppermute | solution.py:28
  42.1 59.9 %copy-start = (bf16[1,16,7168]{2,1,0:T(8,128)(2,1)S(1)}, bf16[1,16,7168]{2,1,0:T(8,128)(2,1)}, u32[]{:S(2)}) copy-start(bf16[1,16,7168]{2,1,0:T(8,128)(2,1)} %param.9) | copy-start | bytes 688132
  42.2 1.9 %collective-permute-start.24 = (bf16[4,8,7168]{2,1,0:T(8,128)(2,1)S(1)}, bf16[4,8,7168]{2,1,0:T(8,128)(2,1)S(1)}, u32[]{:S(2)}, u32[]{:S(2)}) collective-permute-start(bf16[4,8,7168]{2,1,0:T(8,128)(2,1)S(1)} %slice_bitcast_fusion.9), channel_id=1, source_target_pairs={{0,1},{1,0},{2,3},{3,2},{4,5},{5,4},{6,7},{7,6},{8,9},{9,8},{10,11... | collective-permute-start | bytes 1376264 | tf_op jit(solution)/shard_map/ppermute | solution.py:28
  44.2 5.3 %collective-permute-start.25 = (bf16[8,7168]{1,0:T(8,128)(2,1)S(1)}, bf16[8,7168]{1,0:T(8,128)(2,1)S(1)}, u32[]{:S(2)}, u32[]{:S(2)}) collective-permute-start(bf16[8,7168]{1,0:T(8,128)(2,1)S(1)} %get-tuple-element.253), channel_id=1, source_target_pairs={{0,2},{1,3},{2,0},{3,1},{4,6},{5,7},{6,4},{7,5},{8,10},{9,11},{10,... | collective-permute-start | bytes 344072 | tf_op jit(solution)/shard_map/ppermute | solution.py:28
  45.3 8.3 %collective-permute-start.27 = (bf16[8,7168]{1,0:T(8,128)(2,1)S(1)}, bf16[8,7168]{1,0:T(8,128)(2,1)S(1)}, u32[]{:S(2)}, u32[]{:S(2)}) collective-permute-start(bf16[8,7168]{1,0:T(8,128)(2,1)S(1)} %get-tuple-element.254), channel_id=1, source_target_pairs={{0,6},{1,7},{2,4},{3,5},{4,2},{5,3},{6,0},{7,1},{8,14},{9,15},{10,... | collective-permute-start | bytes 344072 | tf_op jit(solution)/shard_map/ppermute | solution.py:28
  47.2 10.8 %collective-permute-start.26 = (bf16[8,7168]{1,0:T(8,128)(2,1)S(1)}, bf16[8,7168]{1,0:T(8,128)(2,1)S(1)}, u32[]{:S(2)}, u32[]{:S(2)}) collective-permute-start(bf16[8,7168]{1,0:T(8,128)(2,1)S(1)} %get-tuple-element.255), channel_id=1, source_target_pairs={{0,4},{1,5},{2,6},{3,7},{4,0},{5,1},{6,2},{7,3},{8,12},{9,13},{10,... | collective-permute-start | bytes 344072 | tf_op jit(solution)/shard_map/ppermute | solution.py:28
  58.2 43.3 %collective-permute-start.30 = (bf16[2,7168]{1,0:T(2,128)(2,1)S(1)}, bf16[2,7168]{1,0:T(2,128)(2,1)S(1)}, u32[]{:S(2)}, u32[]{:S(2)}) collective-permute-start(bf16[2,7168]{1,0:T(2,128)(2,1)S(1)} %get-tuple-element.261), channel_id=1, source_target_pairs={{0,24},{8,16},{16,8},{24,0},{1,25},{9,17},{17,9},{25,1},{2,26},{10... | collective-permute-start | bytes 86024 | tf_op jit(solution)/shard_map/ppermute | solution.py:28
  60.7 40.8 %collective-permute-start.29 = (bf16[2,7168]{1,0:T(2,128)(2,1)S(1)}, bf16[2,7168]{1,0:T(2,128)(2,1)S(1)}, u32[]{:S(2)}, u32[]{:S(2)}) collective-permute-start(bf16[2,7168]{1,0:T(2,128)(2,1)S(1)} %get-tuple-element.262), channel_id=1, source_target_pairs={{0,16},{8,24},{16,0},{24,8},{1,17},{9,25},{17,1},{25,9},{2,18},{10... | collective-permute-start | bytes 86024 | tf_op jit(solution)/shard_map/ppermute | solution.py:28
  61.2 40.3 %collective-permute-start.28 = (bf16[2,7168]{1,0:T(2,128)(2,1)S(1)}, bf16[2,7168]{1,0:T(2,128)(2,1)S(1)}, u32[]{:S(2)}, u32[]{:S(2)}) collective-permute-start(bf16[2,7168]{1,0:T(2,128)(2,1)S(1)} %get-tuple-element.263), channel_id=1, source_target_pairs={{0,8},{8,0},{16,24},{24,16},{1,9},{9,1},{17,25},{25,17},{2,10},{10... | collective-permute-start | bytes 86024 | tf_op jit(solution)/shard_map/ppermute | solution.py:28
  105.1 4.8 %collective-permute-start = (bf16[2,7168]{1,0:T(2,128)(2,1)S(1)}, bf16[2,7168]{1,0:T(2,128)(2,1)S(1)}, u32[]{:S(2)}, u32[]{:S(2)}) collective-permute-start(bf16[2,7168]{1,0:T(2,128)(2,1)S(1)} %get-tuple-element.399), channel_id=1, source_target_pairs={{0,24},{8,16},{16,8},{24,0},{1,25},{9,17},{17,9},{25,1},{2,26},{10... | collective-permute-start | bytes 86024 | tf_op jit(solution)/shard_map/while/body/ppermute | solution.py:28
  107.7 3.9 %collective-permute-start.1 = (bf16[2,7168]{1,0:T(2,128)(2,1)S(1)}, bf16[2,7168]{1,0:T(2,128)(2,1)S(1)}, u32[]{:S(2)}, u32[]{:S(2)}) collective-permute-start(bf16[2,7168]{1,0:T(2,128)(2,1)S(1)} %get-tuple-element.400), channel_id=1, source_target_pairs={{0,16},{8,24},{16,0},{24,8},{1,17},{9,25},{17,1},{25,9},{2,18},{10... | collective-permute-start | bytes 86024 | tf_op jit(solution)/shard_map/while/body/ppermute | solution.py:28
  108.9 3.9 %collective-permute-start.2 = (bf16[2,7168]{1,0:T(2,128)(2,1)S(1)}, bf16[2,7168]{1,0:T(2,128)(2,1)S(1)}, u32[]{:S(2)}, u32[]{:S(2)}) collective-permute-start(bf16[2,7168]{1,0:T(2,128)(2,1)S(1)} %get-tuple-element.401), channel_id=1, source_target_pairs={{0,8},{8,0},{16,24},{24,16},{1,9},{9,1},{17,25},{25,17},{2,10},{10... | collective-permute-start | bytes 86024 | tf_op jit(solution)/shard_map/while/body/ppermute | solution.py:28
  113.6 6.9 %collective-permute-start.5 = (bf16[8,7168]{1,0:T(8,128)(2,1)S(1)}, bf16[8,7168]{1,0:T(8,128)(2,1)S(1)}, u32[]{:S(2)}, u32[]{:S(2)}) collective-permute-start(bf16[8,7168]{1,0:T(8,128)(2,1)S(1)} %multiply_convert_fusion.13), channel_id=1, source_target_pairs={{0,6},{1,7},{2,4},{3,5},{4,2},{5,3},{6,0},{7,1},{8,14},{9,15},{10,... | collective-permute-start | bytes 344072 | tf_op jit(solution)/shard_map/while/body/ppermute | solution.py:28
  115.2 9.4 %collective-permute-start.4 = (bf16[8,7168]{1,0:T(8,128)(2,1)S(1)}, bf16[8,7168]{1,0:T(8,128)(2,1)S(1)}, u32[]{:S(2)}, u32[]{:S(2)}) collective-permute-start(bf16[8,7168]{1,0:T(8,128)(2,1)S(1)} %multiply_convert_fusion.13), channel_id=1, source_target_pairs={{0,4},{1,5},{2,6},{3,7},{4,0},{5,1},{6,2},{7,3},{8,12},{9,13},{10,... | collective-permute-start | bytes 344072 | tf_op jit(solution)/shard_map/while/body/ppermute | solution.py:28
  117.2 7.3 %collective-permute-start.3 = (bf16[8,7168]{1,0:T(8,128)(2,1)S(1)}, bf16[8,7168]{1,0:T(8,128)(2,1)S(1)}, u32[]{:S(2)}, u32[]{:S(2)}) collective-permute-start(bf16[8,7168]{1,0:T(8,128)(2,1)S(1)} %multiply_convert_fusion.13), channel_id=1, source_target_pairs={{0,2},{1,3},{2,0},{3,1},{4,6},{5,7},{6,4},{7,5},{8,10},{9,11},{10,... | collective-permute-start | bytes 344072 | tf_op jit(solution)/shard_map/while/body/ppermute | solution.py:28
  124.6 1.9 %collective-permute-start.6 = (bf16[4,8,7168]{2,1,0:T(8,128)(2,1)S(1)}, bf16[4,8,7168]{2,1,0:T(8,128)(2,1)S(1)}, u32[]{:S(2)}, u32[]{:S(2)}) collective-permute-start(bf16[4,8,7168]{2,1,0:T(8,128)(2,1)S(1)} %pad_maximum_fusion.14), channel_id=1, source_target_pairs={{0,1},{1,0},{2,3},{3,2},{4,5},{5,4},{6,7},{7,6},{8,9},{9,8},{10,11... | collective-permute-start | bytes 1376264 | tf_op jit(solution)/shard_map/while/body/ppermute | solution.py:28
  134.8 1.9 %collective-permute-start.7 = (bf16[4,8,7168]{2,1,0:T(8,128)(2,1)S(1)}, bf16[4,8,7168]{2,1,0:T(8,128)(2,1)S(1)}, u32[]{:S(2)}, u32[]{:S(2)}) collective-permute-start(bf16[4,8,7168]{2,1,0:T(8,128)(2,1)S(1)} %slice_bitcast_fusion.28), channel_id=1, source_target_pairs={{0,1},{1,0},{2,3},{3,2},{4,5},{5,4},{6,7},{7,6},{8,9},{9,8},{10,11... | collective-permute-start | bytes 1376264 | tf_op jit(solution)/shard_map/while/body/ppermute | solution.py:28
  136.8 8.0 %collective-permute-start.8 = (bf16[8,7168]{1,0:T(8,128)(2,1)S(1)}, bf16[8,7168]{1,0:T(8,128)(2,1)S(1)}, u32[]{:S(2)}, u32[]{:S(2)}) collective-permute-start(bf16[8,7168]{1,0:T(8,128)(2,1)S(1)} %get-tuple-element.407), channel_id=1, source_target_pairs={{0,6},{1,7},{2,4},{3,5},{4,2},{5,3},{6,0},{7,1},{8,14},{9,15},{10,... | collective-permute-start | bytes 344072 | tf_op jit(solution)/shard_map/while/body/ppermute | solution.py:28
  138.7 10.1 %collective-permute-start.9 = (bf16[8,7168]{1,0:T(8,128)(2,1)S(1)}, bf16[8,7168]{1,0:T(8,128)(2,1)S(1)}, u32[]{:S(2)}, u32[]{:S(2)}) collective-permute-start(bf16[8,7168]{1,0:T(8,128)(2,1)S(1)} %get-tuple-element.408), channel_id=1, source_target_pairs={{0,4},{1,5},{2,6},{3,7},{4,0},{5,1},{6,2},{7,3},{8,12},{9,13},{10,... | collective-permute-start | bytes 344072 | tf_op jit(solution)/shard_map/while/body/ppermute | solution.py:28
  138.7 10.1 %collective-permute-start.10 = (bf16[8,7168]{1,0:T(8,128)(2,1)S(1)}, bf16[8,7168]{1,0:T(8,128)(2,1)S(1)}, u32[]{:S(2)}, u32[]{:S(2)}) collective-permute-start(bf16[8,7168]{1,0:T(8,128)(2,1)S(1)} %get-tuple-element.409), channel_id=1, source_target_pairs={{0,2},{1,3},{2,0},{3,1},{4,6},{5,7},{6,4},{7,5},{8,10},{9,11},{10,... | collective-permute-start | bytes 344072 | tf_op jit(solution)/shard_map/while/body/ppermute | solution.py:28
  149.0 4.9 %collective-permute-start.11 = (bf16[2,7168]{1,0:T(2,128)(2,1)S(1)}, bf16[2,7168]{1,0:T(2,128)(2,1)S(1)}, u32[]{:S(2)}, u32[]{:S(2)}) collective-permute-start(bf16[2,7168]{1,0:T(2,128)(2,1)S(1)} %get-tuple-element.410), channel_id=1, source_target_pairs={{0,24},{8,16},{16,8},{24,0},{1,25},{9,17},{17,9},{25,1},{2,26},{10... | collective-permute-start | bytes 86024 | tf_op jit(solution)/shard_map/while/body/ppermute | solution.py:28
  150.2 3.9 %collective-permute-start.12 = (bf16[2,7168]{1,0:T(2,128)(2,1)S(1)}, bf16[2,7168]{1,0:T(2,128)(2,1)S(1)}, u32[]{:S(2)}, u32[]{:S(2)}) collective-permute-start(bf16[2,7168]{1,0:T(2,128)(2,1)S(1)} %get-tuple-element.411), channel_id=1, source_target_pairs={{0,16},{8,24},{16,0},{24,8},{1,17},{9,25},{17,1},{25,9},{2,18},{10... | collective-permute-start | bytes 86024 | tf_op jit(solution)/shard_map/while/body/ppermute | solution.py:28
  150.9 3.9 %collective-permute-start.13 = (bf16[2,7168]{1,0:T(2,128)(2,1)S(1)}, bf16[2,7168]{1,0:T(2,128)(2,1)S(1)}, u32[]{:S(2)}, u32[]{:S(2)}) collective-permute-start(bf16[2,7168]{1,0:T(2,128)(2,1)S(1)} %get-tuple-element.412), channel_id=1, source_target_pairs={{0,8},{8,0},{16,24},{24,16},{1,9},{9,1},{17,25},{25,17},{2,10},{10... | collective-permute-start | bytes 86024 | tf_op jit(solution)/shard_map/while/body/ppermute | solution.py:28
  (1 other events, 59.9 us)

commit v2 on v1

--- a/solution.py
+++ b/solution.py
@@ -1,6 +1,10 @@
+import functools
+
 import jax
 import jax.numpy as jnp
 from jax import lax
+from jax.experimental import pallas as pl
+from jax.experimental.pallas import tpu as pltpu
 from jax.sharding import PartitionSpec as P
 
 CAP = 2
@@ -35,21 +39,12 @@
 def dispatch(rows):
     experts, count, width = rows.shape
     n_dev = lax.axis_size("expert")
-    if n_dev == 8:
-        own = rows[0]
-        near = jnp.stack([own] + [swap(own, "expert", 2 * k) for k in range(1, 4)])
-        return jnp.concatenate([near, swap(near, "expert", 1)])
     send = jnp.repeat(rows, n_dev // experts, axis=0)
     return lax.all_to_all(send, "expert", split_axis=0, concat_axis=0, tiled=True)
 
 
 def collect(partial, experts):
     n_dev, count, width = partial.shape
-    if n_dev == 8:
-        other = swap(partial[4:], "expert", 1)
-        both = (partial[:4].astype(jnp.float32) + other.astype(jnp.float32)).astype(jnp.bfloat16)
-        got = [both[0]] + [swap(both[k], "expert", 2 * k) for k in range(1, 4)]
-        return sum(g.astype(jnp.float32) for g in got)[None]
     back = lax.all_to_all(partial, "expert", split_axis=0, concat_axis=0, tiled=True)
     back = back.reshape(experts, n_dev // experts, count, width)
     return jnp.sum(back.astype(jnp.float32), axis=1)
@@ -79,7 +74,7 @@
     return section_exchange([total[k] for k in range(micros)])
 
 
-def shards(embedded, norm_gain, gate_proj, up_proj, down_proj, expert_ids, route_gates):
+def shards_general(embedded, norm_gain, gate_proj, up_proj, down_proj, expert_ids, route_gates):
     n_section = lax.axis_size("section")
     n_dev = lax.axis_size("expert")
     num_experts = n_dev // min(8, n_dev)
@@ -135,6 +130,223 @@
     for layer in range(n_section):
         rows = advance(rows, layer, updates[layer])
     return rows[None]
+
+
+LANES = 128
+BF16 = jnp.bfloat16
+F32 = jnp.float32
+
+
+def prepare_first(width, picks, x0, x1, x2, x3, gain, rows_out, normed_out):
+    messages = (x0, x1, x2, x3)
+    rows = sum(
+        jnp.dot(picks[j], messages[j][:, :width], preferred_element_type=F32) for j in range(4)
+    )
+    rows_out[...] = rows.astype(BF16)
+    mean = jnp.mean(rows * rows, axis=-1, keepdims=True)
+    normed_out[:, :width] = (rows * lax.rsqrt(mean + eps_norm) * gain[...]).astype(BF16)
+    lane = lax.broadcasted_iota(jnp.int32, (x0.shape[0], LANES), 1)
+    slots = 4 * CAP
+    count = sum(jnp.where(m[:, width:].astype(F32) > 0, 1.0, 0.0) for m in messages)
+    count = jnp.where(lane < slots, count, 0.0)
+    pair = jnp.where(lane % CAP == 0, count + pltpu.roll(count, LANES - 1, 1), 0.0)
+    deepest = jnp.max(jnp.max(pair, axis=1, keepdims=True), axis=0, keepdims=True)
+    normed_out[:, width:] = jnp.broadcast_to(deepest, (rows.shape[0], LANES)).astype(BF16)
+
+
+def prepare_next(place, coef, base, updates, gain, normed_out):
+    rows = base[...].astype(F32)
+    count = rows.shape[0]
+    for layer in range(coef.shape[0]):
+        step = updates[place[0] ^ layer].astype(F32)
+        change = (
+            coef[layer, 0] * step
+            + coef[layer, 1] * pltpu.roll(step, count - 1, 0)
+            + coef[layer, 2] * pltpu.roll(step, 1, 0)
+        )
+        rows = (rows + change).astype(BF16).astype(F32)
+    mean = jnp.mean(rows * rows, axis=-1, keepdims=True)
+    normed_out[...] = (rows * lax.rsqrt(mean + eps_norm) * gain[...]).astype(BF16)
+
+
+def finish(place, weights, base, updates, out):
+    rows = base[0].astype(F32)
+    for layer in range(weights.shape[0]):
+        step = updates[place[0] ^ layer].astype(F32)
+        change = sum(weights[layer, q] * step[q : q + 1] for q in range(step.shape[0]))
+        rows = (rows + change).astype(BF16).astype(F32)
+    out[0] = rows.astype(BF16)
+
+
+CHUNKS = 7
+
+
+def expert_kernel(near, far, gate, up, down, near_out, far_out, rows, gates, ups, downs, sems):
+    half, width = near_out.shape
+    part = width // CHUNKS
+    copies = []
+    for c in range(CHUNKS):
+        span = pl.ds(c * part, part)
+        copies.append(pltpu.make_async_copy(gate.at[0, span], gates.at[span], sems.at[0, c]))
+        copies.append(pltpu.make_async_copy(up.at[0, span], ups.at[span], sems.at[1, c]))
+    for c in range(CHUNKS):
+        span = pl.ds(c * part, part)
+        copies.append(
+            pltpu.make_async_copy(down.at[0, :, span], downs.at[:, span], sems.at[2, c])
+        )
+    for copy in copies:
+        copy.start()
+    rows[:half] = near[:, :width]
+    rows[half:] = far[:, :width]
+    gate_val = up_val = 0.0
+    for c in range(CHUNKS):
+        span = pl.ds(c * part, part)
+        piece = rows[:, span]
+        copies[2 * c].wait()
+        gate_val += jnp.dot(piece, gates[span], preferred_element_type=F32)
+        copies[2 * c + 1].wait()
+        up_val += jnp.dot(piece, ups[span], preferred_element_type=F32)
+    hidden = (gate_val * jax.nn.sigmoid(gate_val) * up_val).astype(BF16)
+    for c in range(CHUNKS):
+        span = pl.ds(c * part, part)
+        copies[2 * CHUNKS + c].wait()
+        value = jnp.dot(hidden, downs[:, span], preferred_element_type=F32).astype(BF16)
+        near_out[:, span] = value[:half]
+        far_out[:, span] = value[half:]
+
+
+VMEM = pl.BlockSpec(memory_space=pltpu.VMEM)
+SMEM = pl.BlockSpec(memory_space=pltpu.SMEM)
+HBM = pl.BlockSpec(memory_space=pl.ANY)
+
+
+def expert_call(near, far, gate, up, down):
+    half = near.shape[0]
+    _, width, hidden = gate.shape
+    out = jax.ShapeDtypeStruct((half, width), BF16)
+    return pl.pallas_call(
+        expert_kernel,
+        out_shape=(out, out),
+        in_specs=[VMEM, VMEM, HBM, HBM, HBM],
+        out_specs=(VMEM, VMEM),
+        scratch_shapes=[
+            pltpu.VMEM((2 * half, width), BF16),
+            pltpu.VMEM((width, hidden), BF16),
+            pltpu.VMEM((width, hidden), BF16),
+            pltpu.VMEM((hidden, width), BF16),
+            pltpu.SemaphoreType.DMA((3, CHUNKS)),
+        ],
+        compiler_params=pltpu.CompilerParams(vmem_limit_bytes=32 * 2**20),
+        cost_estimate=pl.CostEstimate(
+            flops=12 * half * width * hidden,
+            bytes_accessed=6 * width * hidden,
+            transcendentals=2 * half * hidden,
+        ),
+        name="experts",
+    )(near, far, gate, up, down)
+
+
+def spread(array):
+    return [array] + [swap(array, "section", j) for j in range(1, 4)]
+
+
+def group_rows(normed):
+    near = jnp.concatenate([normed] + [swap(normed, "expert", 2 * k) for k in range(1, 4)])
+    return near, swap(near, "expert", 1)
+
+
+def group_sum(near, far, count):
+    other = swap(far, "expert", 1)
+    both = (near.astype(F32) + other.astype(F32)).astype(BF16)
+    parts = [both[k * count : (k + 1) * count] for k in range(4)]
+    got = [parts[0]] + [swap(parts[k], "expert", 2 * k) for k in range(1, 4)]
+    return sum(g.astype(F32) for g in got).astype(BF16)
+
+
+def shards_group(embedded, norm_gain, gate_proj, up_proj, down_proj, expert_ids, route_gates):
+    me = lax.axis_index("section")
+    place = me.astype(jnp.int32)[None]
+    tokens, width = embedded.shape[1:]
+    micros = expert_ids.shape[1]
+    count = micros * CAP
+    own = slot_weights(expert_ids[0], route_gates[0], 1)
+    flat = own.transpose(1, 0, 2).reshape(tokens, count)
+    high = lax.reduce_precision(flat, 8, 7)
+    middle = lax.reduce_precision(flat - high, 8, 7)
+    parts = jnp.concatenate([high, middle, flat - high - middle], axis=1).astype(BF16)
+    parts = jnp.pad(parts, ((0, 0), (0, LANES - 3 * count)))
+    messages = spread(jnp.concatenate([embedded[0], parts], axis=1))
+
+    chosen = (own > 0).astype(BF16)
+    spot = jnp.eye(micros, dtype=BF16)
+    selector = spot[:, :, None, None] * chosen.transpose(0, 2, 1)[:, None]
+    selector = selector.reshape(micros, count, tokens)
+    picks = jnp.stack(
+        [lax.dynamic_index_in_dim(selector, me ^ j, 0, keepdims=False) for j in range(4)]
+    )
+    rows, normed = pl.pallas_call(
+        functools.partial(prepare_first, width),
+        out_shape=(
+            jax.ShapeDtypeStruct((count, width), BF16),
+            jax.ShapeDtypeStruct((count, width + LANES), BF16),
+        ),
+        in_specs=[VMEM] * 6,
+        out_specs=(VMEM, VMEM),
+        compiler_params=pltpu.CompilerParams(vmem_limit_bytes=32 * 2**20),
+        name="prepare_first",
+    )(picks, *messages, norm_gain)
+
+    def rest(normed):
+        near, far = group_rows(normed)
+        near_part, far_part = expert_call(near, far, gate_proj, up_proj, down_proj)
+        update = group_sum(near_part, far_part, count)
+        return near, far, jnp.stack(spread(update))
+
+    near, far, updates = rest(normed)
+    depth = jnp.maximum(jnp.max(near[:, width:]), jnp.max(far[:, width:])).astype(jnp.int32)
+
+    tables = jnp.stack([m[:, width : width + 3 * count] for m in messages]).astype(F32)
+    tables = tables.reshape(4, tokens, 3, micros, CAP)
+    tables = (tables[:, :, 0] + tables[:, :, 1] + tables[:, :, 2]).transpose(0, 2, 1, 3)
+    tables = jnp.stack(
+        [lax.dynamic_index_in_dim(tables, me ^ l, 0, keepdims=False) for l in range(4)]
+    )
+    cross = jnp.sum(
+        (own > 0).astype(F32)[None, :, :, :, None] * tables[:, :, :, None, :], axis=2
+    )
+    cross = jnp.where(jnp.arange(4)[:, None, None, None] < me, cross, 0.0)[:3]
+    same = jnp.stack([cross[:, :, 0, 0], cross[:, :, 1, 1]], axis=-1)
+    nothing = jnp.zeros_like(same[..., 0])
+    after = jnp.stack([cross[:, :, 0, 1], nothing], axis=-1)
+    before = jnp.stack([nothing, cross[:, :, 1, 0]], axis=-1)
+    coef = jnp.stack([same, after, before], axis=1).reshape(3, 3, count, 1)
+
+    def body(state):
+        done, updates = state
+        normed = pl.pallas_call(
+            prepare_next,
+            out_shape=jax.ShapeDtypeStruct((count, width), BF16),
+            in_specs=[SMEM] + [VMEM] * 4,
+            out_specs=VMEM,
+            compiler_params=pltpu.CompilerParams(vmem_limit_bytes=32 * 2**20),
+            name="prepare_next",
+        )(place, coef, rows, updates, norm_gain)
+        return done + 1, rest(normed)[2]
+
+    _, updates = lax.while_loop(lambda s: s[0] < depth, body, (jnp.int32(1), updates))
+    mine = lax.dynamic_index_in_dim(tables, me, 1, keepdims=False)
+    weights = (
+        (jnp.arange(micros) == me).astype(F32)[None, :, None, None]
+        * mine.transpose(0, 2, 1)[:, None]
+    ).reshape(4, count, tokens, 1)
+    return pl.pallas_call(
+        finish,
+        out_shape=jax.ShapeDtypeStruct(embedded.shape, BF16),
+        in_specs=[SMEM] + [VMEM] * 3,
+        out_specs=VMEM,
+        compiler_params=pltpu.CompilerParams(vmem_limit_bytes=32 * 2**20),
+        name="finish",
+    )(place, weights, embedded, updates)
 
 
 def solution(mesh):
@@ -147,6 +359,7 @@
         P("section", None, "expert", None),
         P("section", None, "expert", None),
     )
+    fits = mesh.shape["expert"] == 8 and mesh.shape["section"] == 4
     return jax.shard_map(
-        shards, mesh=mesh, in_specs=placed, out_specs=P("section", "expert", None), check_vma=False
-    )
+        shards_group if fits else shards_general, mesh=mesh, in_specs=placed, out_specs=P("section", "expert", None), check_vma=False
+    )

time: 159 us -> 112 us (0.70)
  blocking collectives: 39 us -> 0 us
  matrix products: 25.1 us -> 0 us
  Pallas kernels: 0 us -> 16.1 us
  waiting for transfers between devices: 47.1 us -> 57.6 us
  starting transfers between devices: 37.1 us -> 29.2 us
  loops' own time: 1.78 us -> 0.09 us
  other arithmetic: 6.53 us -> 4.91 us
    pmax x1 -> x0, blocking collectives: 39 us -> none  [shards(): depth = lax.pmax(jnp.max(picks), ('section', 'expert'))]
    dot_general x18 -> x0, matrix products: 25.1 us -> none  [the longest x2 10.9 us: expert_block(): jnp.dot(hidden, down_mat, preferred_element_type=jnp.float32)]
    pallas_call x0 -> x5, Pallas kernels: none -> 16.1 us  [the longest x2 11 us: expert_call(): pl.pallas_call(expert_kernel, out_shape=(out, out), in_specs=[VMEM, VMEM,...]
    ppermute x31 -> x25, waiting for transfers between devices: 47.1 us -> 57.6 us  [swap(): return lax.ppermute(array, axis, [(i, i ^ by) for i in range(devices)])]
    ppermute x31 -> x25, starting transfers between devices: 37.1 us -> 29.2 us  [swap(): return lax.ppermute(array, axis, [(i, i ^ by) for i in range(devices)])]
    another operation x1, loops' own time: 1.78 us -> 0.09 us  [shards_group(): lax.while_loop(lambda s: s[0] < depth, body, (jnp.int32(1), updates))]
  transfers between devices with their start and end apart: 31 -> 25, of which waited for: 25 -> 21; matrix products, arithmetic and copies ran while one was open for 1% -> 3% of each run, Pallas kernels for 0% -> 0%
where the time goes in v2:
time: 112 us; the launch traced here: 111 us
  waiting for transfers between devices  57.6 us (51%)
  starting transfers between devices  29.2 us (26%)
  Pallas kernels  16.1 us (14%)
  other arithmetic  4.91 us (4%)
  local copies, waits for them, and re-layouts  1.91 us (2%)
  between operations  1.59 us (1%)
    ppermute x25, waiting for transfers between devices, swap(): return lax.ppermute(array, axis, [(i, i ^ by) for i in range(devices)])  57.6 us
    ppermute x25, starting transfers between devices, swap(): return lax.ppermute(array, axis, [(i, i ^ by) for i in range(devices)])  29.2 us
    pallas_call x2, Pallas kernels, expert_call(): pl.pallas_call(expert_kernel, out_shape=(out, out), in_specs=[VMEM, VMEM,...  11 us
    pallas_call x1, Pallas kernels, shards_group(): pl.pallas_call(finish, out_shape=jax.ShapeDtypeStruct(embedded.shape, BF1...  3.4 us
  transfers between devices with their start and end apart: 25, of which 21 were waited for; matrix products, arithmetic and copies ran while one was open for 3% of the time, Pallas kernels for 0%

profile of v2, /device:TPU:0, one launch (start us, length us, event | category | flops | bytes accessed | tf_op | source)
XLA Modules:
  0.0 111.4 jit_solution(11751467172920142136)
XLA Ops:
  2.9 4.0 %collective-permute-start.13 = (bf16[16,7296]{1,0:T(8,128)(2,1)S(1)}, bf16[16,7296]{1,0:T(8,128)(2,1)S(1)}, u32[]{:S(2)}, u32[]{:S(2)}) collective-permute-start(bf16[16,7296]{1,0:T(8,128)(2,1)S(1)} %pad_maximum_fusion.3.x0), channel_id=1, source_target_pairs={{0,24},{8,16},{16,8},{24,0},{1,25},{9,17},{17,9},{25,1},{2,26},{10... | collective-permute-start | bytes 700424 | tf_op jit(solution)/shard_map/ppermute | solution.py:32
  8.0 5.5 %collective-permute-done.13.x3 = bf16[16,7296]{1,0:T(8,128)(2,1)S(1)} collective-permute-done((bf16[16,7296]{1,0:T(8,128)(2,1)S(1)}, bf16[16,7296]{1,0:T(8,128)(2,1)S(1)}, u32[]{:S(2)}, u32[]{:S(2)}) %collective-permute-start.13) | collective-permute-done | bytes 233504 | tf_op jit(solution)/shard_map/ppermute | solution.py:32
  13.5 4.1 %collective-permute-done.12.x2 = bf16[16,7296]{1,0:T(8,128)(2,1)S(1)} collective-permute-done((bf16[16,7296]{1,0:T(8,128)(2,1)S(1)}, bf16[16,7296]{1,0:T(8,128)(2,1)S(1)}, u32[]{:S(2)}, u32[]{:S(2)}) %collective-permute-start.12) | collective-permute-done | bytes 233504 | tf_op jit(solution)/shard_map/ppermute | solution.py:32
  17.9 1.2 %prepare_first.1 = (bf16[8,7168]{1,0:T(8,128)(2,1)S(1)}, bf16[8,7296]{1,0:T(8,128)(2,1)S(1)}) custom-call(bf16[4,8,16]{2,1,0:T(8,128)(2,1)S(1)} %pad_maximum_fusion.5.picks, bf16[16,7296]{1,0:T(8,128)(2,1)S(1)} %pad_maximum_fusion.3.x0, bf16[16,7296]{1,0:T(8,128)(2,1)S(1)} %collective-permute-done.11.x1, bf16[16,7296]{1,0:T(8,128)(2,1)S(1)} %collective-permute-done.12.x2, ...), custom_call_target="tpu_custom_call" | custom-call | tf_op jit(solution)/shard_map/prepare_first/pallas_call | solution.py:287
  19.1 3.7 %collective-permute-start.16 = (bf16[8,7296]{1,0:T(8,128)(2,1)S(1)}, bf16[8,7296]{1,0:T(8,128)(2,1)S(1)}, u32[]{:S(2)}, u32[]{:S(2)}) collective-permute-start(bf16[8,7296]{1,0:T(8,128)(2,1)S(1)} %get-tuple-element.64), channel_id=1, source_target_pairs={{0,6},{1,7},{2,4},{3,5},{4,2},{5,3},{6,0},{7,1},{8,14},{9,15},{10,... | collective-permute-start | bytes 350216 | tf_op jit(solution)/shard_map/ppermute | solution.py:32
  24.0 6.4 %collective-permute-done.14 = bf16[8,7296]{1,0:T(8,128)(2,1)S(1)} collective-permute-done((bf16[8,7296]{1,0:T(8,128)(2,1)S(1)}, bf16[8,7296]{1,0:T(8,128)(2,1)S(1)}, u32[]{:S(2)}, u32[]{:S(2)}) %collective-permute-start.14) | collective-permute-done | bytes 116768 | tf_op jit(solution)/shard_map/ppermute | solution.py:32
  30.4 2.3 %collective-permute-done.15 = bf16[8,7296]{1,0:T(8,128)(2,1)S(1)} collective-permute-done((bf16[8,7296]{1,0:T(8,128)(2,1)S(1)}, bf16[8,7296]{1,0:T(8,128)(2,1)S(1)}, u32[]{:S(2)}, u32[]{:S(2)}) %collective-permute-start.15) | collective-permute-done | bytes 116768 | tf_op jit(solution)/shard_map/ppermute | solution.py:32
  33.4 1.3 %collective-permute-done.17.far = bf16[32,7296]{1,0:T(8,128)(2,1)S(1)} collective-permute-done((bf16[32,7296]{1,0:T(8,128)(2,1)S(1)}, bf16[32,7296]{1,0:T(8,128)(2,1)S(1)}, u32[]{:S(2)}, u32[]{:S(2)}) %collective-permute-start.17) | collective-permute-done | bytes 466976 | tf_op jit(solution)/shard_map/ppermute | solution.py:32
  34.7 5.5 %experts.2 = (bf16[32,7168]{1,0:T(8,128)(2,1)S(1)}, bf16[32,7168]{1,0:T(8,128)(2,1)S(1)}) custom-call(bf16[32,7296]{1,0:T(8,128)(2,1)S(1)} %constant_dynamic-update-slice_fusion.near, bf16[32,7296]{1,0:T(8,128)(2,1)S(1)} %collective-permute-done.17.far, bf16[1,7168,256]{2,1,0:T(8,128)(2,1)} %gate.1, bf16[1,7168,256]{2,1,0:T(8,128)(2,1)} %up.1, ...), custom_call_target="tpu_custom_call" | custom-call | flops 704643072 | bytes 11010048 | tf_op jit(solution)/shard_map/experts/pallas_call | solution.py:227
  40.5 1.6 %collective-permute-done.18 = bf16[32,7168]{1,0:T(8,128)(2,1)S(1)} collective-permute-done((bf16[32,7168]{1,0:T(8,128)(2,1)S(1)}, bf16[32,7168]{1,0:T(8,128)(2,1)S(1)}, u32[]{:S(2)}, u32[]{:S(2)}) %collective-permute-start.18) | collective-permute-done | bytes 458784 | tf_op jit(solution)/shard_map/ppermute | solution.py:32
  42.4 2.4 %collective-permute-start.21 = (bf16[8,7168]{1,0:T(8,128)(2,1)S(1)}, bf16[8,7168]{1,0:T(8,128)(2,1)S(1)}, u32[]{:S(2)}, u32[]{:S(2)}) collective-permute-start(bf16[8,7168]{1,0:T(8,128)(2,1)S(1)} %get-tuple-element.147), channel_id=1, source_target_pairs={{0,6},{1,7},{2,4},{3,5},{4,2},{5,3},{6,0},{7,1},{8,14},{9,15},{10,... | collective-permute-start | bytes 344072 | tf_op jit(solution)/shard_map/ppermute | solution.py:32
  47.5 3.8 %collective-permute-done.21 = bf16[8,7168]{1,0:T(8,128)(2,1)S(1)} collective-permute-done((bf16[8,7168]{1,0:T(8,128)(2,1)S(1)}, bf16[8,7168]{1,0:T(8,128)(2,1)S(1)}, u32[]{:S(2)}, u32[]{:S(2)}) %collective-permute-start.21) | collective-permute-done | bytes 114720 | tf_op jit(solution)/shard_map/ppermute | solution.py:32
  51.2 4.8 %collective-permute-done.20 = bf16[8,7168]{1,0:T(8,128)(2,1)S(1)} collective-permute-done((bf16[8,7168]{1,0:T(8,128)(2,1)S(1)}, bf16[8,7168]{1,0:T(8,128)(2,1)S(1)}, u32[]{:S(2)}, u32[]{:S(2)}) %collective-permute-start.20) | collective-permute-done | bytes 114720 | tf_op jit(solution)/shard_map/ppermute | solution.py:32
  57.1 2.0 %collective-permute-start.23 = (bf16[8,7168]{1,0:T(8,128)(2,1)S(1)}, bf16[8,7168]{1,0:T(8,128)(2,1)S(1)}, u32[]{:S(2)}, u32[]{:S(2)}) collective-permute-start(bf16[8,7168]{1,0:T(8,128)(2,1)S(1)} %add_convert_fusion.3), channel_id=1, source_target_pairs={{0,16},{8,24},{16,0},{24,8},{1,17},{9,25},{17,1},{25,9},{2,18},{10... | collective-permute-start | bytes 344072 | tf_op jit(solution)/shard_map/ppermute | solution.py:32
  62.8 1.2 %collective-permute-done.23 = bf16[8,7168]{1,0:T(8,128)(2,1)S(1)} collective-permute-done((bf16[8,7168]{1,0:T(8,128)(2,1)S(1)}, bf16[8,7168]{1,0:T(8,128)(2,1)S(1)}, u32[]{:S(2)}, u32[]{:S(2)}) %collective-permute-start.23) | collective-permute-done | bytes 114720 | tf_op jit(solution)/shard_map/ppermute | solution.py:32
  64.3 43.7 %while.10 = (s32[]{:T(128)}, bf16[4,8,7168]{2,1,0:T(8,128)(2,1)S(1)}, s32[]{:T(128)}, s32[1]{0:T(128)}, f32[3,3,8,1]{3,2,1,0:T(8,128)S(1)}, /*index=5*/bf16[8,71...) while((s32[]{:T(128)}, ...), condition=%wide.region_7.8_spmd, body=%wide.region_6.7_spmd.sunk | while | flops 708542464 | bytes 23282212 | solution.py:336
  64.9 2.8 %collective-permute-start.1 = (bf16[8,7168]{1,0:T(8,128)(2,1)S(1)}, bf16[8,7168]{1,0:T(8,128)(2,1)S(1)}, u32[]{:S(2)}, u32[]{:S(2)}) collective-permute-start(bf16[8,7168]{1,0:T(8,128)(2,1)S(1)} %prepare_next.1), channel_id=1, source_target_pairs={{0,4},{1,5},{2,6},{3,7},{4,0},{5,1},{6,2},{7,3},{8,12},{9,13},{10,... | collective-permute-start | bytes 344072 | tf_op jit(solution)/shard_map/while/body/ppermute | solution.py:32
  67.7 1.6 %collective-permute-start = (bf16[8,7168]{1,0:T(8,128)(2,1)S(1)}, bf16[8,7168]{1,0:T(8,128)(2,1)S(1)}, u32[]{:S(2)}, u32[]{:S(2)}) collective-permute-start(bf16[8,7168]{1,0:T(8,128)(2,1)S(1)} %prepare_next.1), channel_id=1, source_target_pairs={{0,6},{1,7},{2,4},{3,5},{4,2},{5,3},{6,0},{7,1},{8,14},{9,15},{10,... | collective-permute-start | bytes 344072 | tf_op jit(solution)/shard_map/while/body/ppermute | solution.py:32
  69.3 1.6 %collective-permute-done.2 = bf16[8,7168]{1,0:T(8,128)(2,1)S(1)} collective-permute-done((bf16[8,7168]{1,0:T(8,128)(2,1)S(1)}, bf16[8,7168]{1,0:T(8,128)(2,1)S(1)}, u32[]{:S(2)}, u32[]{:S(2)}) %collective-permute-start.2) | collective-permute-done | bytes 114720 | tf_op jit(solution)/shard_map/while/body/ppermute | solution.py:32
  70.9 5.6 %collective-permute-done.1 = bf16[8,7168]{1,0:T(8,128)(2,1)S(1)} collective-permute-done((bf16[8,7168]{1,0:T(8,128)(2,1)S(1)}, bf16[8,7168]{1,0:T(8,128)(2,1)S(1)}, u32[]{:S(2)}, u32[]{:S(2)}) %collective-permute-start.1) | collective-permute-done | bytes 114720 | tf_op jit(solution)/shard_map/while/body/ppermute | solution.py:32
  76.6 1.8 %collective-permute-done.3.far = bf16[32,7168]{1,0:T(8,128)(2,1)S(1)} collective-permute-done((bf16[32,7168]{1,0:T(8,128)(2,1)S(1)}, bf16[32,7168]{1,0:T(8,128)(2,1)S(1)}, u32[]{:S(2)}, u32[]{:S(2)}) %collective-permute-start.3) | collective-permute-done | bytes 458784 | tf_op jit(solution)/shard_map/while/body/ppermute | solution.py:32
  78.4 5.5 %experts.3 = (bf16[32,7168]{1,0:T(8,128)(2,1)S(1)}, bf16[32,7168]{1,0:T(8,128)(2,1)S(1)}) custom-call(bf16[32,7168]{1,0:T(8,128)(2,1)S(1)} %pad_maximum_fusion.10.near, bf16[32,7168]{1,0:T(8,128)(2,1)S(1)} %collective-permute-done.3.far, bf16[1,7168,256]{2,1,0:T(8,128)(2,1)} %get-tuple-element.269.gate, bf16[1,7168,256]{2,1,0:T(8,128)(2,1)} %get-tuple-element.270.up, ...), custom_call_target="tpu_custom_call" | custom-call | flops 704643072 | bytes 11010048 | tf_op jit(solution)/shard_map/while/body/experts/pallas_call | solution.py:227
  84.1 1.7 %collective-permute-done.4 = bf16[32,7168]{1,0:T(8,128)(2,1)S(1)} collective-permute-done((bf16[32,7168]{1,0:T(8,128)(2,1)S(1)}, bf16[32,7168]{1,0:T(8,128)(2,1)S(1)}, u32[]{:S(2)}, u32[]{:S(2)}) %collective-permute-start.4) | collective-permute-done | bytes 458784 | tf_op jit(solution)/shard_map/while/body/ppermute | solution.py:32
  86.0 2.0 %collective-permute-start.5 = (bf16[8,7168]{1,0:T(8,128)(2,1)S(1)}, bf16[8,7168]{1,0:T(8,128)(2,1)S(1)}, u32[]{:S(2)}, u32[]{:S(2)}) collective-permute-start(bf16[8,7168]{1,0:T(8,128)(2,1)S(1)} %get-tuple-element.237), channel_id=1, source_target_pairs={{0,6},{1,7},{2,4},{3,5},{4,2},{5,3},{6,0},{7,1},{8,14},{9,15},{10,... | collective-permute-start | bytes 344072 | tf_op jit(solution)/shard_map/while/body/ppermute | solution.py:32
  87.9 1.4 %collective-permute-start.6 = (bf16[8,7168]{1,0:T(8,128)(2,1)S(1)}, bf16[8,7168]{1,0:T(8,128)(2,1)S(1)}, u32[]{:S(2)}, u32[]{:S(2)}) collective-permute-start(bf16[8,7168]{1,0:T(8,128)(2,1)S(1)} %get-tuple-element.238), channel_id=1, source_target_pairs={{0,4},{1,5},{2,6},{3,7},{4,0},{5,1},{6,2},{7,3},{8,12},{9,13},{10,... | collective-permute-start | bytes 344072 | tf_op jit(solution)/shard_map/while/body/ppermute | solution.py:32
  90.4 3.5 %collective-permute-done.5 = bf16[8,7168]{1,0:T(8,128)(2,1)S(1)} collective-permute-done((bf16[8,7168]{1,0:T(8,128)(2,1)S(1)}, bf16[8,7168]{1,0:T(8,128)(2,1)S(1)}, u32[]{:S(2)}, u32[]{:S(2)}) %collective-permute-start.5) | collective-permute-done | bytes 114720 | tf_op jit(solution)/shard_map/while/body/ppermute | solution.py:32
  93.9 5.9 %collective-permute-done.6 = bf16[8,7168]{1,0:T(8,128)(2,1)S(1)} collective-permute-done((bf16[8,7168]{1,0:T(8,128)(2,1)S(1)}, bf16[8,7168]{1,0:T(8,128)(2,1)S(1)}, u32[]{:S(2)}, u32[]{:S(2)}) %collective-permute-start.6) | collective-permute-done | bytes 114720 | tf_op jit(solution)/shard_map/while/body/ppermute | solution.py:32
  99.9 1.3 %collective-permute-start.10 = (bf16[8,7168]{1,0:T(8,128)(2,1)S(1)}, bf16[8,7168]{1,0:T(8,128)(2,1)S(1)}, u32[]{:S(2)}, u32[]{:S(2)}) collective-permute-start(bf16[8,7168]{1,0:T(8,128)(2,1)S(1)} %add_convert_fusion.7), channel_id=1, source_target_pairs={{0,8},{8,0},{16,24},{24,16},{1,9},{9,1},{17,25},{25,17},{2,10},{10... | collective-permute-start | bytes 344072 | tf_op jit(solution)/shard_map/while/body/ppermute | solution.py:32
  101.4 2.0 %collective-permute-start.8 = (bf16[8,7168]{1,0:T(8,128)(2,1)S(1)}, bf16[8,7168]{1,0:T(8,128)(2,1)S(1)}, u32[]{:S(2)}, u32[]{:S(2)}) collective-permute-start(bf16[8,7168]{1,0:T(8,128)(2,1)S(1)} %add_convert_fusion.7), channel_id=1, source_target_pairs={{0,24},{8,16},{16,8},{24,0},{1,25},{9,17},{17,9},{25,1},{2,26},{10... | collective-permute-start | bytes 344072 | tf_op jit(solution)/shard_map/while/body/ppermute | solution.py:32
  103.4 2.0 %collective-permute-done.10 = bf16[8,7168]{1,0:T(8,128)(2,1)S(1)} collective-permute-done((bf16[8,7168]{1,0:T(8,128)(2,1)S(1)}, bf16[8,7168]{1,0:T(8,128)(2,1)S(1)}, u32[]{:S(2)}, u32[]{:S(2)}) %collective-permute-start.10) | collective-permute-done | bytes 114720 | tf_op jit(solution)/shard_map/while/body/ppermute | solution.py:32
  105.4 2.5 %collective-permute-done.9 = bf16[8,7168]{1,0:T(8,128)(2,1)S(1)} collective-permute-done((bf16[8,7168]{1,0:T(8,128)(2,1)S(1)}, bf16[8,7168]{1,0:T(8,128)(2,1)S(1)}, u32[]{:S(2)}, u32[]{:S(2)}) %collective-permute-start.9) | collective-permute-done | bytes 114720 | tf_op jit(solution)/shard_map/while/body/ppermute | solution.py:32
  108.0 3.4 %finish.1 = bf16[1,16,7168]{2,1,0:T(8,128)(2,1)} custom-call(s32[1]{0:T(128)} %bitcast.4.place, f32[4,8,16,1]{3,2,1,0:T(8,128)S(1)} %broadcast_multiply_fusion.weights, bf16[1,16,7168]{2,1,0:T(8,128)(2,1)S(1)} %copy-done, bf16[4,8,7168]{2,1,0:T(8,128)(2,1)S(1)} %get-tuple-element.68.updates), custom_call_target="tpu_custom_call" | custom-call | tf_op jit(solution)/shard_map/finish/pallas_call | solution.py:342
  (103 shorter events, 15.5 us)
Async XLA Ops:
  2.9 10.5 %collective-permute-start.13 = (bf16[16,7296]{1,0:T(8,128)(2,1)S(1)}, bf16[16,7296]{1,0:T(8,128)(2,1)S(1)}, u32[]{:S(2)}, u32[]{:S(2)}) collective-permute-start(bf16[16,7296]{1,0:T(8,128)(2,1)S(1)} %pad_maximum_fusion.3.x0), channel_id=1, source_target_pairs={{0,24},{8,16},{16,8},{24,0},{1,25},{9,17},{17,9},{25,1},{2,26},{10... | collective-permute-start | bytes 700424 | tf_op jit(solution)/shard_map/ppermute | solution.py:32
  6.9 10.7 %collective-permute-start.12 = (bf16[16,7296]{1,0:T(8,128)(2,1)S(1)}, bf16[16,7296]{1,0:T(8,128)(2,1)S(1)}, u32[]{:S(2)}, u32[]{:S(2)}) collective-permute-start(bf16[16,7296]{1,0:T(8,128)(2,1)S(1)} %pad_maximum_fusion.3.x0), channel_id=1, source_target_pairs={{0,16},{8,24},{16,0},{24,8},{1,17},{9,25},{17,1},{25,9},{2,18},{10... | collective-permute-start | bytes 700424 | tf_op jit(solution)/shard_map/ppermute | solution.py:32
  7.4 10.5 %collective-permute-start.11 = (bf16[16,7296]{1,0:T(8,128)(2,1)S(1)}, bf16[16,7296]{1,0:T(8,128)(2,1)S(1)}, u32[]{:S(2)}, u32[]{:S(2)}) collective-permute-start(bf16[16,7296]{1,0:T(8,128)(2,1)S(1)} %pad_maximum_fusion.3.x0), channel_id=1, source_target_pairs={{0,8},{8,0},{16,24},{24,16},{1,9},{9,1},{17,25},{25,17},{2,10},{10... | collective-permute-start | bytes 700424 | tf_op jit(solution)/shard_map/ppermute | solution.py:32
  19.1 13.6 %collective-permute-start.16 = (bf16[8,7296]{1,0:T(8,128)(2,1)S(1)}, bf16[8,7296]{1,0:T(8,128)(2,1)S(1)}, u32[]{:S(2)}, u32[]{:S(2)}) collective-permute-start(bf16[8,7296]{1,0:T(8,128)(2,1)S(1)} %get-tuple-element.64), channel_id=1, source_target_pairs={{0,6},{1,7},{2,4},{3,5},{4,2},{5,3},{6,0},{7,1},{8,14},{9,15},{10,... | collective-permute-start | bytes 350216 | tf_op jit(solution)/shard_map/ppermute | solution.py:32
  22.8 9.9 %collective-permute-start.15 = (bf16[8,7296]{1,0:T(8,128)(2,1)S(1)}, bf16[8,7296]{1,0:T(8,128)(2,1)S(1)}, u32[]{:S(2)}, u32[]{:S(2)}) collective-permute-start(bf16[8,7296]{1,0:T(8,128)(2,1)S(1)} %get-tuple-element.64), channel_id=1, source_target_pairs={{0,4},{1,5},{2,6},{3,7},{4,0},{5,1},{6,2},{7,3},{8,12},{9,13},{10,... | collective-permute-start | bytes 350216 | tf_op jit(solution)/shard_map/ppermute | solution.py:32
  22.8 7.6 %collective-permute-start.14 = (bf16[8,7296]{1,0:T(8,128)(2,1)S(1)}, bf16[8,7296]{1,0:T(8,128)(2,1)S(1)}, u32[]{:S(2)}, u32[]{:S(2)}) collective-permute-start(bf16[8,7296]{1,0:T(8,128)(2,1)S(1)} %get-tuple-element.64), channel_id=1, source_target_pairs={{0,2},{1,3},{2,0},{3,1},{4,6},{5,7},{6,4},{7,5},{8,10},{9,11},{10,... | collective-permute-start | bytes 350216 | tf_op jit(solution)/shard_map/ppermute | solution.py:32
  32.8 1.9 %collective-permute-start.17 = (bf16[32,7296]{1,0:T(8,128)(2,1)S(1)}, bf16[32,7296]{1,0:T(8,128)(2,1)S(1)}, u32[]{:S(2)}, u32[]{:S(2)}) collective-permute-start(bf16[32,7296]{1,0:T(8,128)(2,1)S(1)} %constant_dynamic-update-slice_fusion.near), channel_id=1, source_target_pairs={{0,1},{1,0},{2,3},{3,2},{4,5},{5,4},{6,7},{7,6},{8,9},{9,8},{10,11... | collective-permute-start | bytes 1400840 | tf_op jit(solution)/shard_map/ppermute | solution.py:32
  40.2 24.1 %copy-start.1 = (f32[1,7168]{1,0:T(1,128)S(1)}, f32[1,7168]{1,0:T(1,128)}, u32[]{:S(2)}) copy-start(f32[1,7168]{1,0:T(1,128)} %gain.1) | copy-start | bytes 86020
  40.2 1.9 %collective-permute-start.18 = (bf16[32,7168]{1,0:T(8,128)(2,1)S(1)}, bf16[32,7168]{1,0:T(8,128)(2,1)S(1)}, u32[]{:S(2)}, u32[]{:S(2)}) collective-permute-start(bf16[32,7168]{1,0:T(8,128)(2,1)S(1)} %get-tuple-element.66), channel_id=1, source_target_pairs={{0,1},{1,0},{2,3},{3,2},{4,5},{5,4},{6,7},{7,6},{8,9},{9,8},{10,11... | collective-permute-start | bytes 1376264 | tf_op jit(solution)/shard_map/ppermute | solution.py:32
  42.2 5.3 %collective-permute-start.19 = (bf16[8,7168]{1,0:T(8,128)(2,1)S(1)}, bf16[8,7168]{1,0:T(8,128)(2,1)S(1)}, u32[]{:S(2)}, u32[]{:S(2)}) collective-permute-start(bf16[8,7168]{1,0:T(8,128)(2,1)S(1)} %get-tuple-element.146), channel_id=1, source_target_pairs={{0,2},{1,3},{2,0},{3,1},{4,6},{5,7},{6,4},{7,5},{8,10},{9,11},{10,... | collective-permute-start | bytes 344072 | tf_op jit(solution)/shard_map/ppermute | solution.py:32
  42.4 8.8 %collective-permute-start.21 = (bf16[8,7168]{1,0:T(8,128)(2,1)S(1)}, bf16[8,7168]{1,0:T(8,128)(2,1)S(1)}, u32[]{:S(2)}, u32[]{:S(2)}) collective-permute-start(bf16[8,7168]{1,0:T(8,128)(2,1)S(1)} %get-tuple-element.147), channel_id=1, source_target_pairs={{0,6},{1,7},{2,4},{3,5},{4,2},{5,3},{6,0},{7,1},{8,14},{9,15},{10,... | collective-permute-start | bytes 344072 | tf_op jit(solution)/shard_map/ppermute | solution.py:32
  44.8 11.2 %collective-permute-start.20 = (bf16[8,7168]{1,0:T(8,128)(2,1)S(1)}, bf16[8,7168]{1,0:T(8,128)(2,1)S(1)}, u32[]{:S(2)}, u32[]{:S(2)}) collective-permute-start(bf16[8,7168]{1,0:T(8,128)(2,1)S(1)} %get-tuple-element.148), channel_id=1, source_target_pairs={{0,4},{1,5},{2,6},{3,7},{4,0},{5,1},{6,2},{7,3},{8,12},{9,13},{10,... | collective-permute-start | bytes 344072 | tf_op jit(solution)/shard_map/ppermute | solution.py:32
  56.1 6.7 %collective-permute-start.24 = (bf16[8,7168]{1,0:T(8,128)(2,1)S(1)}, bf16[8,7168]{1,0:T(8,128)(2,1)S(1)}, u32[]{:S(2)}, u32[]{:S(2)}) collective-permute-start(bf16[8,7168]{1,0:T(8,128)(2,1)S(1)} %add_convert_fusion.3), channel_id=1, source_target_pairs={{0,24},{8,16},{16,8},{24,0},{1,25},{9,17},{17,9},{25,1},{2,26},{10... | collective-permute-start | bytes 344072 | tf_op jit(solution)/shard_map/ppermute | solution.py:32
  57.1 6.8 %collective-permute-start.23 = (bf16[8,7168]{1,0:T(8,128)(2,1)S(1)}, bf16[8,7168]{1,0:T(8,128)(2,1)S(1)}, u32[]{:S(2)}, u32[]{:S(2)}) collective-permute-start(bf16[8,7168]{1,0:T(8,128)(2,1)S(1)} %add_convert_fusion.3), channel_id=1, source_target_pairs={{0,16},{8,24},{16,0},{24,8},{1,17},{9,25},{17,1},{25,9},{2,18},{10... | collective-permute-start | bytes 344072 | tf_op jit(solution)/shard_map/ppermute | solution.py:32
  59.1 5.1 %collective-permute-start.22 = (bf16[8,7168]{1,0:T(8,128)(2,1)S(1)}, bf16[8,7168]{1,0:T(8,128)(2,1)S(1)}, u32[]{:S(2)}, u32[]{:S(2)}) collective-permute-start(bf16[8,7168]{1,0:T(8,128)(2,1)S(1)} %add_convert_fusion.3), channel_id=1, source_target_pairs={{0,8},{8,0},{16,24},{24,16},{1,9},{9,1},{17,25},{25,17},{2,10},{10... | collective-permute-start | bytes 344072 | tf_op jit(solution)/shard_map/ppermute | solution.py:32
  64.3 43.7 %copy-start = (bf16[1,16,7168]{2,1,0:T(8,128)(2,1)S(1)}, bf16[1,16,7168]{2,1,0:T(8,128)(2,1)}, u32[]{:S(2)}) copy-start(bf16[1,16,7168]{2,1,0:T(8,128)(2,1)} %base.1) | copy-start | bytes 688132
  64.8 6.1 %collective-permute-start.2 = (bf16[8,7168]{1,0:T(8,128)(2,1)S(1)}, bf16[8,7168]{1,0:T(8,128)(2,1)S(1)}, u32[]{:S(2)}, u32[]{:S(2)}) collective-permute-start(bf16[8,7168]{1,0:T(8,128)(2,1)S(1)} %prepare_next.1), channel_id=1, source_target_pairs={{0,2},{1,3},{2,0},{3,1},{4,6},{5,7},{6,4},{7,5},{8,10},{9,11},{10,... | collective-permute-start | bytes 344072 | tf_op jit(solution)/shard_map/while/body/ppermute | solution.py:32
  64.9 11.6 %collective-permute-start.1 = (bf16[8,7168]{1,0:T(8,128)(2,1)S(1)}, bf16[8,7168]{1,0:T(8,128)(2,1)S(1)}, u32[]{:S(2)}, u32[]{:S(2)}) collective-permute-start(bf16[8,7168]{1,0:T(8,128)(2,1)S(1)} %prepare_next.1), channel_id=1, source_target_pairs={{0,4},{1,5},{2,6},{3,7},{4,0},{5,1},{6,2},{7,3},{8,12},{9,13},{10,... | collective-permute-start | bytes 344072 | tf_op jit(solution)/shard_map/while/body/ppermute | solution.py:32
  67.7 8.8 %collective-permute-start = (bf16[8,7168]{1,0:T(8,128)(2,1)S(1)}, bf16[8,7168]{1,0:T(8,128)(2,1)S(1)}, u32[]{:S(2)}, u32[]{:S(2)}) collective-permute-start(bf16[8,7168]{1,0:T(8,128)(2,1)S(1)} %prepare_next.1), channel_id=1, source_target_pairs={{0,6},{1,7},{2,4},{3,5},{4,2},{5,3},{6,0},{7,1},{8,14},{9,15},{10,... | collective-permute-start | bytes 344072 | tf_op jit(solution)/shard_map/while/body/ppermute | solution.py:32
  76.5 1.9 %collective-permute-start.3 = (bf16[32,7168]{1,0:T(8,128)(2,1)S(1)}, bf16[32,7168]{1,0:T(8,128)(2,1)S(1)}, u32[]{:S(2)}, u32[]{:S(2)}) collective-permute-start(bf16[32,7168]{1,0:T(8,128)(2,1)S(1)} %pad_maximum_fusion.10.near), channel_id=1, source_target_pairs={{0,1},{1,0},{2,3},{3,2},{4,5},{5,4},{6,7},{7,6},{8,9},{9,8},{10,11... | collective-permute-start | bytes 1376264 | tf_op jit(solution)/shard_map/while/body/ppermute | solution.py:32
  83.9 1.9 %collective-permute-start.4 = (bf16[32,7168]{1,0:T(8,128)(2,1)S(1)}, bf16[32,7168]{1,0:T(8,128)(2,1)S(1)}, u32[]{:S(2)}, u32[]{:S(2)}) collective-permute-start(bf16[32,7168]{1,0:T(8,128)(2,1)S(1)} %get-tuple-element.235), channel_id=1, source_target_pairs={{0,1},{1,0},{2,3},{3,2},{4,5},{5,4},{6,7},{7,6},{8,9},{9,8},{10,11... | collective-permute-start | bytes 1376264 | tf_op jit(solution)/shard_map/while/body/ppermute | solution.py:32
  86.0 8.0 %collective-permute-start.5 = (bf16[8,7168]{1,0:T(8,128)(2,1)S(1)}, bf16[8,7168]{1,0:T(8,128)(2,1)S(1)}, u32[]{:S(2)}, u32[]{:S(2)}) collective-permute-start(bf16[8,7168]{1,0:T(8,128)(2,1)S(1)} %get-tuple-element.237), channel_id=1, source_target_pairs={{0,6},{1,7},{2,4},{3,5},{4,2},{5,3},{6,0},{7,1},{8,14},{9,15},{10,... | collective-permute-start | bytes 344072 | tf_op jit(solution)/shard_map/while/body/ppermute | solution.py:32
  87.9 11.9 %collective-permute-start.6 = (bf16[8,7168]{1,0:T(8,128)(2,1)S(1)}, bf16[8,7168]{1,0:T(8,128)(2,1)S(1)}, u32[]{:S(2)}, u32[]{:S(2)}) collective-permute-start(bf16[8,7168]{1,0:T(8,128)(2,1)S(1)} %get-tuple-element.238), channel_id=1, source_target_pairs={{0,4},{1,5},{2,6},{3,7},{4,0},{5,1},{6,2},{7,3},{8,12},{9,13},{10,... | collective-permute-start | bytes 344072 | tf_op jit(solution)/shard_map/while/body/ppermute | solution.py:32
  89.3 10.5 %collective-permute-start.7 = (bf16[8,7168]{1,0:T(8,128)(2,1)S(1)}, bf16[8,7168]{1,0:T(8,128)(2,1)S(1)}, u32[]{:S(2)}, u32[]{:S(2)}) collective-permute-start(bf16[8,7168]{1,0:T(8,128)(2,1)S(1)} %get-tuple-element.239), channel_id=1, source_target_pairs={{0,2},{1,3},{2,0},{3,1},{4,6},{5,7},{6,4},{7,5},{8,10},{9,11},{10,... | collective-permute-start | bytes 344072 | tf_op jit(solution)/shard_map/while/body/ppermute | solution.py:32
  99.9 5.5 %collective-permute-start.10 = (bf16[8,7168]{1,0:T(8,128)(2,1)S(1)}, bf16[8,7168]{1,0:T(8,128)(2,1)S(1)}, u32[]{:S(2)}, u32[]{:S(2)}) collective-permute-start(bf16[8,7168]{1,0:T(8,128)(2,1)S(1)} %add_convert_fusion.7), channel_id=1, source_target_pairs={{0,8},{8,0},{16,24},{24,16},{1,9},{9,1},{17,25},{25,17},{2,10},{10... | collective-permute-start | bytes 344072 | tf_op jit(solution)/shard_map/while/body/ppermute | solution.py:32
  101.2 6.8 %collective-permute-start.9 = (bf16[8,7168]{1,0:T(8,128)(2,1)S(1)}, bf16[8,7168]{1,0:T(8,128)(2,1)S(1)}, u32[]{:S(2)}, u32[]{:S(2)}) collective-permute-start(bf16[8,7168]{1,0:T(8,128)(2,1)S(1)} %add_convert_fusion.7), channel_id=1, source_target_pairs={{0,16},{8,24},{16,0},{24,8},{1,17},{9,25},{17,1},{25,9},{2,18},{10... | collective-permute-start | bytes 344072 | tf_op jit(solution)/shard_map/while/body/ppermute | solution.py:32
  101.4 6.5 %collective-permute-start.8 = (bf16[8,7168]{1,0:T(8,128)(2,1)S(1)}, bf16[8,7168]{1,0:T(8,128)(2,1)S(1)}, u32[]{:S(2)}, u32[]{:S(2)}) collective-permute-start(bf16[8,7168]{1,0:T(8,128)(2,1)S(1)} %add_convert_fusion.7), channel_id=1, source_target_pairs={{0,24},{8,16},{16,8},{24,0},{1,25},{9,17},{17,9},{25,1},{2,26},{10... | collective-permute-start | bytes 344072 | tf_op jit(solution)/shard_map/while/body/ppermute | solution.py:32
